TPU v7x, 256 devices: a whole 4x4x8 slice. The times are simulated.
256 devices in a mesh: member: 8 (over z_hi, x), dp: 32 (over z_lo, y, core).
Axes of the slice: x: 4, y: 4, z: 8 (z_hi: 2, z_lo: 4; z = z_hi * 4 + z_lo), core: 2. Of those that a mesh axis runs over, the one named last changes fastest.
Arguments:
- acts: bfloat16 [32, 8, 48, 4096], P('dp', 'member'), may hold values from -6 to 6
- base: bfloat16 [32, 8, 48, 4608], P('dp', 'member'), may hold values from -6 to 6
- down_matrices: bfloat16 [8, 4096, 128], P('member'), may hold values from -0.09375 to 0.09375
- up_matrices: bfloat16 [8, 4608, 128], P('member'), may hold values from -0.5 to 0.5
- head: bfloat16 [8, 4608], P('member'), may hold values from -0.359375 to 0.359375
- gain: float32 [4608], replicated, may hold values from 0.25 to 1.75
- lengths: int32 [32, 4], P('dp'), may hold values from 1 to 192, 384 in all within a row
- pairing: int32 [128], replicated, may hold values from 0 to 127, each once
Outputs:
- loss: float32 [8], P('member')
- grad_a: float32 [8, 4096, 128], P('member', 'dp')
- grad_b: float32 [8, 4608, 128], P('member', 'dp')
Inputs may be any that keep to these rules, and one draw needn't show every extreme that they name: Each row of lengths sums to 384; its largest entry is 192. pairing names every response exactly once.
All inputs are finite; a program needn't handle non-finite values.
Results may differ from a plain program's by a relative error of at most 0.0041.
Values may be sent and summed in bfloat16 or wider, within the bound.
A program may use at most 64 MiB of HBM per device.

v0:
```python
import jax
import jax.numpy as jnp
from jax import lax
from jax.sharding import PartitionSpec as P


def per_device(acts, base, down_matrices, up_matrices, head, gain, lengths, pairing):
    whole_acts, whole_base = (
        lax.all_gather(acts, "member", axis=1, tiled=True),
        lax.all_gather(base, "member", axis=1, tiled=True),
    )
    shard = whole_acts.shape[1] * whole_acts.shape[2]
    width_e = whole_acts.shape[3]
    width_d = whole_base.shape[3]
    flat_acts = whole_acts.reshape(shard, width_e)
    flat_base = whole_base.reshape(shard, width_d).astype(jnp.float32)
    adapter_down = down_matrices[0]
    adapter_up = up_matrices[0]
    head_vec = head[0].astype(jnp.float32)
    own_lengths = lengths[0]
    resp_dev = own_lengths.shape[0]
    ends = jnp.cumsum(own_lengths)
    starts = ends - own_lengths
    position = jnp.arange(shard, dtype=jnp.int32)
    member_of = (
        (position[None, :] >= starts[:, None]) & (position[None, :] < ends[:, None])
    ).astype(jnp.float32)
    inverse_len = 1.0 / own_lengths.astype(jnp.float32)
    low = jnp.dot(flat_acts, adapter_down, preferred_element_type=jnp.float32).astype(jnp.bfloat16)
    y_full = flat_base + lax.dot_general(
        low, adapter_up, (((1,), (1,)), ((), ())), preferred_element_type=jnp.float32
    )
    scale = lax.rsqrt(jnp.mean(y_full * y_full, axis=1, keepdims=True) + 1e-06)
    normed = y_full * scale * gain[None, :]
    score = jnp.sum(normed * head_vec[None, :], axis=1)
    reward = jnp.sum(member_of * score[None, :], axis=1) * inverse_len
    every_reward = lax.all_gather(reward, "dp", axis=0, tiled=True)
    resp_all = every_reward.shape[0]
    select = (pairing[:, None] == jnp.arange(resp_all, dtype=jnp.int32)[None, :]).astype(
        jnp.float32
    )
    ordered = jnp.sum(select * every_reward[None, :], axis=1)
    margin = ordered[0::2] - ordered[1::2]
    loss = jnp.mean(jax.nn.softplus(-margin)).reshape(1)
    slope = -jax.nn.sigmoid(-margin)
    coef = jnp.stack([slope, -slope], axis=1).reshape(resp_all)
    dreward_all = jnp.sum(select * coef[:, None], axis=0)
    dreward = (
        lax.dynamic_slice_in_dim(dreward_all, lax.axis_index("dp") * resp_dev, resp_dev)
        * inverse_len
    )
    dscore = jnp.sum(dreward[:, None] * member_of, axis=0)
    grad_z = dscore[:, None] * head_vec[None, :] * gain[None, :]
    inner = jnp.mean(grad_z * y_full, axis=1, keepdims=True)
    grad_y = (scale * (grad_z - scale * scale * y_full * inner)).astype(jnp.bfloat16)
    grad_low = jnp.dot(grad_y, adapter_up, preferred_element_type=jnp.float32).astype(jnp.bfloat16)
    groups = lax.axis_size("dp")
    rows_a = width_e // groups
    rows_b = width_d // groups
    term_a = lax.dot_general(
        flat_acts, grad_low, (((0,), (0,)), ((), ())), preferred_element_type=jnp.float32
    )
    term_b = lax.dot_general(
        grad_y, low, (((0,), (0,)), ((), ())), preferred_element_type=jnp.float32
    )
    total_a, total_b = lax.psum((term_a, term_b), "dp")
    place = lax.axis_index("dp")
    grad_a = lax.dynamic_slice_in_dim(total_a, place * rows_a, rows_a, 0)
    grad_b = lax.dynamic_slice_in_dim(total_b, place * rows_b, rows_b, 0)
    return (loss, grad_a[None], grad_b[None])


def solution(mesh):
    return jax.shard_map(
        per_device,
        mesh=mesh,
        in_specs=(
            P("dp", "member", None, None),
            P("dp", "member", None, None),
            P("member", None, None),
            P("member", None, None),
            P("member", None),
            P(),
            P("dp", None),
            P(),
        ),
        out_specs=(P("member"), P("member", "dp", None), P("member", "dp", None)),
        check_vma=False,
    )
```

profile of v0, /device:TPU:1, one launch (start us, length us, event | category | flops | bytes accessed | tf_op | source)
XLA Modules:
  0.0 591.5 jit_solution(17755099081530545829)
XLA Ops:
  7.2 0.7 all-gather.5.cloned.1.call-update
  8.0 0.7 all-gather.3.cloned.1.call-update
  8.7 0.8 reduce-window.7
  9.5 1.3 dynamic-slice
  11.5 0.8 convert_reduce_fusion
  12.2 0.7 bitcast_subtract_fusion
  12.9 92.9 %all-gather.5.cloned.1.call-done = bf16[1,8,48,4096]{3,2,0,1:T(8,128)(2,1)} async-done(((bf16[1,1,48,4096]{3,2,0,1:T(8,128)(2,1)}), bf16[1,8,48,4096]{3,2,0,1:T(8,128)(2,1)}) %all-gather.5.cloned.1.call-update) | async-done | bytes 3145744 | tf_op jit(solution)/shard_map/all_gather | solution.py:9
  105.8 3.1 convolution_convert_fusion
  109.0 92.2 %all-gather.3.cloned.1.call-done = bf16[1,8,48,4608]{3,2,0,1:T(8,128)(2,1)} async-done(((bf16[1,1,48,4608]{3,2,0,1:T(8,128)(2,1)}), bf16[1,8,48,4608]{3,2,0,1:T(8,128)(2,1)}) %all-gather.3.cloned.1.call-update) | async-done | bytes 3538960 | tf_op jit(solution)/shard_map/all_gather | solution.py:10
  201.2 3.2 multiply_reduce_fusion.2
  204.4 1.3 multiply_reduce_fusion.1
  205.7 1.6 copy-done.1
  207.3 0.2 select_reduce_fusion.3
  207.6 67.8 %all-reduce = f32[128]{0:T(128)S(1)} all-reduce(f32[128]{0:T(128)S(1)} %get-tuple-element.7), channel_id=1, replica_groups=mesh['member'=8,'dp'=32] {'dp'}, use_global_device_ids=true, to_apply=%add | all-reduce | flops 128 | bytes 1024
  275.9 0.6 negate_bitcast_fusion
  277.1 4.3 multiply_reduce_fusion
  281.4 0.7 copy-done.2
  282.1 3.9 multiply_convert_fusion
  286.0 7.1 %convolution_bitcast_fusion = f32[4096,128]{0,1:T(8,128)} fusion(bf16[384,4096]{1,0:T(8,128)(2,1)} %bitcast.45, bf16[384,4608]{1,0:T(8,128)(2,1)} %multiply_convert_fusion, bf16[1,4608,128]{2,1,0:T(8,128)(2,1)S(1)} %copy-done), kind=kOutput, calls=%fused_computation.6 | convolution fusion | flops 855687168 | bytes 9961472 | tf_op jit(solution)/shard_map/dot_general | solution.py:60
  293.1 4.5 fusion.14
  298.4 282.4 %all-reduce.4.cloned.1.call-done = (f32[4096,128]{0,1:T(8,128)}, f32[4608,128]{1,0:T(8,128)}) async-done(((f32[4096,128]{0,1:T(8,128)}, f32[4608,128]{1,0:T(8,128)}), (f32[4096,128]{0,1:T(8,128)}, f32[4608,128]{1,0:T(8,128)})) %all-reduce.4.cloned.1.call-update) | async-done | bytes 4456464 | tf_op jit(solution)/shard_map/psum | solution.py:66
  580.8 0.8 constant_dynamic-slice_fusion
  581.6 0.7 copy.21
  582.4 1.5 dynamic-slice_bitcast_fusion
  (27 shorter events, 1.3 us)
Async XLA Ops:
  7.2 194.0 %copy-start = (bf16[1,4608,128]{2,1,0:T(8,128)(2,1)S(1)}, bf16[1,4608,128]{2,1,0:T(8,128)(2,1)}, u32[]{:S(2)}) copy-start(bf16[1,4608,128]{2,1,0:T(8,128)(2,1)} %param.11) | copy-start | bytes 3538948
  7.2 98.7 %all-gather.5.cloned.1.call-start = ((), (), s32[]{:S(2)}) async-start(), calls=%async_computation.1 | async-start | bytes 3538944 | tf_op jit(solution)/shard_map/all_gather | solution.py:9
  7.9 193.2 %all-gather.3.cloned.1.call-start = ((), (), s32[]{:S(2)}) async-start(), calls=%async_computation | async-start | bytes 3981312 | tf_op jit(solution)/shard_map/all_gather | solution.py:10
  8.7 572.1 %all-reduce.4.cloned.1.call-start = ((), (), s32[]{:S(2)}) async-start(), calls=%async_computation.2 | async-start | bytes 8912896 | tf_op jit(solution)/shard_map/psum | solution.py:66
  201.2 3.2 copy-start.3
  204.4 2.9 copy-start.1
  204.4 3.1 copy-start.4
  204.4 71.0 %copy-start.5 = (s32[128]{0:T(128)S(1)}, s32[128]{0:T(128)}, u32[]{:S(2)}) copy-start(s32[128]{0:T(128)} %param.15) | copy-start | bytes 1540
  277.1 5.0 copy-start.2
Sparse Core Ops, SparseCore 0:
  10.6 95.1 all-gather.4
  108.4 92.6 all-gather.2
  297.8 282.9 all-reduce.3
where the time goes:
time: 592 us
  waiting for transfers between devices  469 us (79%)
  blocking collectives  67.8 us (11%)
  matrix products  18.1 us (3%)
  between operations  16.3 us (3%)
  other arithmetic  13.1 us (2%)
  local copies, waits for them, and re-layouts  7.23 us (1%)
    psum x1, waiting for transfers between devices, per_device(): total_a, total_b = lax.psum((term_a, term_b), 'dp')  282 us
    all_gather x1, waiting for transfers between devices, per_device(): lax.all_gather(acts, 'member', axis=1, tiled=True)  92.9 us
    all_gather x1, waiting for transfers between devices, per_device(): lax.all_gather(base, 'member', axis=1, tiled=True)  92.2 us
    unnamed x1, blocking collectives  67.8 us
  transfers between devices with their start and end apart: 3, of which 3 were waited for; matrix products, arithmetic and copies ran while one was open for 1% of the time, Pallas kernels for 0%

commit v1 on v0

v1 whole, which is shorter than its diff:
```python
import jax
import jax.numpy as jnp
from jax import lax
from jax.experimental import pallas as pl
from jax.experimental.pallas import tpu as pltpu
from jax.sharding import PartitionSpec as P

F32, BF16, I32 = jnp.float32, jnp.bfloat16, jnp.int32
MESH = pl.DeviceIdType.MESH
HIGH = lax.Precision.HIGHEST

NX, NZH, NZL, NY, NC = 4, 2, 4, 4, 2
NZ = NZH * NZL
TOK = 48
ROWS = NX * TOK
AUG = 16
WA, WB, RANK = 4096, 4608, 128
RA, RB = 128, 144
RAB = RA + RB
RESP = 128
XCH = 2
WAB = WA + WB
ZCH = 8
ZROWS = WAB // 4 // ZCH
ZLAG = NZL - 1
TN = (((0,), (0,)), ((), ()))
NT = (((1,), (1,)), ((), ()))


def dot(a, b, dims=(((1,), (0,)), ((), ())), precision=None):
    return lax.dot_general(a, b, dims, precision=precision, preferred_element_type=F32)


def split(v):
    hi = v.astype(BF16)
    return hi, (v - hi.astype(F32)).astype(BF16)


def kernel(
    acts, base, down, up, head, gain, lengths, pairing,
    loss_ref, ga_ref, gb_ref,
    xa, xb, wv, hv, gv, lv, pv, hpk, hrecv, plow, pt, pbh, pnb, gram, rs1, rs2,
    qa, qb, mbd, tmpa, tmpb, g32, gr, rc, b1, s2a, s2b, sa, sb, b2, fin,
    loc, xs, xr, zs, zr, cs, cr, hs, hr, r1s, r1r, r2s, r2r,
    c1s, c1r, y1s, y1r, y2s, y2r, fs, fr,
):
    me_m, me_d = lax.axis_index("member"), lax.axis_index("dp")
    zh, x = lax.div(me_m, NX), lax.rem(me_m, NX)
    zl = lax.div(me_d, NY * NC)
    yc = lax.rem(me_d, NY * NC)
    y, c = lax.div(yc, NC), lax.rem(yc, NC)
    z = zh * NZL + zl

    def dev(x_, z_, yc_):
        return (lax.div(z_, NZL) * NX + x_, lax.rem(z_, NZL) * (NY * NC) + yc_)

    def remote(src, dst, ssem, rsem, to):
        return pltpu.make_async_remote_copy(
            src_ref=src, dst_ref=dst, send_sem=ssem, recv_sem=rsem, device_id=to, device_id_type=MESH
        )

    right, left = lax.rem(x + 1, NX), lax.rem(x + 3, NX)
    zup, zdown, zother = lax.rem(z + 1, NZ), lax.rem(z + 7, NZ), lax.rem(z + 4, NZ)
    core_peer = dev(x, z, y * NC + 1 - c)

    def load(i):
        return pltpu.make_async_copy(*(
            (head, hv), (gain, gv), (lengths, lv), (pairing, pv),
            (acts.at[0, 0], xa.at[pl.ds(0, TOK)]), (base.at[0, 0], xb.at[pl.ds(0, TOK)]),
            (down.at[0], wv.at[0, pl.ds(0, WA)]), (up.at[0], wv.at[0, pl.ds(WA, WB)]),
        )[i], loc.at[i])

    for i in range(8):
        load(i).start()

    barrier = pltpu.get_barrier_semaphore()
    peers = [dev(right, z, yc), dev(left, z, yc)]
    peers += [dev(x, lax.rem(z + d, NZ), yc) for d in range(1, NZ)]
    peers += [dev(x, z, lax.rem(yc + d, NY * NC)) for d in range(1, NY * NC)]
    for peer in peers:
        pl.semaphore_signal(barrier, inc=1, device_id=peer, device_id_type=MESH)
    pl.semaphore_wait(barrier, len(peers))

    ca, cb = WA // XCH, WB // XCH

    def xpiece(i, slot):
        if i < XCH:
            return xa.at[pl.ds(slot * TOK, TOK), pl.ds(i * ca, ca)]
        return xb.at[pl.ds(slot * TOK, TOK), pl.ds((i - XCH) * cb, cb)]

    def xsource(i):
        if i < XCH:
            return acts.at[0, 0, :, pl.ds(i * ca, ca)]
        return base.at[0, 0, :, pl.ds((i - XCH) * cb, cb)]

    def xcopy(i, way):
        if way == 0:
            return remote(xsource(i), xpiece(i, 1), xs.at[0, i], xr.at[0, i], dev(right, z, yc))
        if way == 1:
            return remote(xsource(i), xpiece(i, 2), xs.at[1, i], xr.at[1, i], dev(left, z, yc))
        onward = lax.rem(x + 1 + 2 * c, NX)
        return remote(xpiece(i, 1 + c), xpiece(i, 3), xs.at[2, i], xr.at[2, i], dev(onward, z, yc))

    def xwait(i, way):
        xcopy(i, way).wait_recv()

    def zrows(s, i, core):
        return pl.ds(pl.multiple_of((2 * s + core) * (WAB // 4) + i * ZROWS, 16), ZROWS)

    def zcopy(s, i, own):
        rows = zrows(s, i, c)
        to = zup if s == 0 else zdown
        return remote(wv.at[0 if own else 1, rows], wv.at[1, rows], zs.at[s, i], zr.at[s, i], dev(x, to, yc))

    def ccopy(s, i, core):
        rows = zrows(s, i, core)
        return remote(wv.at[1, rows], wv.at[1, rows], cs.at[s, i], cr.at[s, i], core_peer)

    for i in range(2 * XCH):
        xcopy(i, 0).start()
        xcopy(i, 1).start()
    load(0).wait()
    for i in range(WB // 128):
        hpk[i : i + 1, :] = hv[0:1, i * 128 : (i + 1) * 128].astype(F32)
    hcopy = remote(hpk, hrecv, hs, hr, dev(x, zother, yc))
    hcopy.start()
    load(6).wait()
    load(7).wait()
    edge = (NZL - 1, 0)
    for s in range(2):
        @pl.when(zl == edge[s])
        def _():
            for i in range(ZCH):
                zcopy(s, i, True).start()

    lag = (jnp.maximum(2 * zl - 3, 0), jnp.maximum(3 - 2 * zl, 0))

    def zstep(t, carry):
        for s in range(2):
            i = t - lag[s]

            @pl.when((i >= 0) & (i < ZCH))
            def _():
                zcopy(s, i, False).wait_recv()

                @pl.when(zl != edge[s])
                def _():
                    zcopy(s, i, False).start()

                ccopy(s, i, c).start()

        return carry

    done = 0
    for i in range(2 * XCH):
        until = (5, 7, 9, ZCH + ZLAG)[i]
        lax.fori_loop(done, until, zstep, 0)
        done = until

        @pl.when(c == 0)
        def _():
            xwait(i, 0)

        @pl.when(c == 1)
        def _():
            xwait(i, 1)

        xcopy(i, 2).start()

    hcopy.wait_recv()
    load(1).wait()
    arow = lax.broadcasted_iota(I32, (AUG, 128), 0)
    for i in range(WB // 128):
        cols = slice(i * 128, (i + 1) * 128)
        g = gv[i : i + 1, :]
        hi0, lo0 = split(hpk[i : i + 1, :] * g)
        hi1, lo1 = split(hrecv[i : i + 1, :] * g)
        tile = jnp.where(arow < 2, hi0.astype(F32), 0.0)
        tile = jnp.where(arow == 2, lo0.astype(F32), tile)
        tile = jnp.where((arow == 3) | (arow == 4), hi1.astype(F32), tile)
        tile = jnp.where(arow == 5, lo1.astype(F32), tile)
        xb[ROWS : ROWS + AUG, cols] = tile.astype(BF16)

    for i in (2, 3, 4, 5):
        load(i).wait()

    def cwait(i, carry):
        for s in range(2):
            ccopy(s, i, 1 - c).wait_recv()
        return carry

    lax.fori_loop(0, ZCH, cwait, 0)

    kb = 512
    gram[...] = jnp.zeros_like(gram)

    def wcat(first, n):
        rows = pl.ds(pl.multiple_of(first, 16), n)
        return jnp.concatenate([wv[0, rows, :], wv[1, rows, :]], axis=1)

    def gram_step(i, uh):
        rows = pl.ds(pl.multiple_of(i * kb, kb), kb)
        u = wcat(WA + i * kb, kb)
        gram[...] += dot(u, u, TN)
        return uh + dot(xb[pl.ds(ROWS, AUG), rows], u)

    uh16 = lax.fori_loop(0, WB // kb, gram_step, jnp.zeros((AUG, 2 * RANK), F32))
    lane2 = lax.broadcasted_iota(I32, (1, 2 * RANK), 1)
    uh = jnp.where(lane2 < RANK, uh16[0:1] + uh16[2:3], uh16[3:4] + uh16[5:6])
    same = (lax.broadcasted_iota(I32, (2 * RANK, 2 * RANK), 0) < RANK) == (
        lax.broadcasted_iota(I32, (2 * RANK, 2 * RANK), 1) < RANK
    )
    gram_hi, gram_lo = split(jnp.where(same, gram[...], 0.0))

    def forward(first, n):
        rows = pl.ds(first, n)

        def step_a(i, acc):
            k = pl.ds(pl.multiple_of(i * kb, kb), kb)
            return acc + dot(xa[rows, k], wcat(i * kb, kb))

        plow[rows, :] = lax.fori_loop(0, WA // kb, step_a, jnp.zeros((n, 2 * RANK), F32))

        def step_b(i, acc):
            t, bh, nb = acc
            k = pl.ds(pl.multiple_of(i * kb, kb), kb)
            block = xb[rows, k]
            wide = block.astype(F32)
            square = wide * wide
            for j in range(kb // 128):
                nb = nb + square[:, j * 128 : (j + 1) * 128]
            return (t + dot(block, wcat(WA + i * kb, kb)), bh + dot(block, xb[pl.ds(ROWS, AUG), k], NT), nb)

        t, bh, nb = lax.fori_loop(
            0,
            WB // kb,
            step_b,
            (jnp.zeros((n, 2 * RANK), F32), jnp.zeros((n, AUG), F32), jnp.zeros((n, 128), F32)),
        )
        pt[rows, :] = t
        pbh[rows, :] = bh
        pnb[rows, :] = nb

    for i in range(2 * XCH):
        @pl.when(c == 0)
        def _():
            xwait(i, 1)

        @pl.when(c == 1)
        def _():
            xwait(i, 0)

    forward(0, 3 * TOK)
    for i in range(2 * XCH):
        xwait(i, 2)
    forward(3 * TOK, TOK)

    low = plow[...].astype(BF16)
    lowf = low.astype(F32)
    yu = pt[...] + dot(low, gram_hi) + dot(low, gram_lo)
    cross = lowf * (pt[...] + yu)
    along = lowf * uh
    nb = jnp.sum(pnb[...], axis=1, keepdims=True)
    bh = pbh[...]
    scale, yh = [], []
    for r in range(2):
        half = slice(r * RANK, (r + 1) * RANK)
        n2 = jnp.maximum(nb + jnp.sum(cross[:, half], axis=1, keepdims=True), 0.0)
        scale.append(lax.rsqrt(n2 * (1.0 / WB) + 1e-06))
        yh.append(
            bh[:, 3 * r : 3 * r + 1]
            + bh[:, 3 * r + 2 : 3 * r + 3]
            + jnp.sum(along[:, half], axis=1, keepdims=True)
        )

    row = lax.broadcasted_iota(I32, (ROWS, RESP), 0)
    slot = jnp.where(row < TOK, 0, jnp.where(row < 2 * TOK, 3, jnp.where(row < 3 * TOK, 1, 2)))
    shift = jnp.where(row < TOK, 0, jnp.where(row < 2 * TOK, 1, jnp.where(row < 3 * TOK, 2, 3)))
    block = x + slot
    block = jnp.where(block >= NX, block - NX, block)
    position = zh * ROWS + block * TOK + row - shift * TOK
    lens = [lv[0, k] for k in range(4)]
    lane = lax.broadcasted_iota(I32, (1, RESP), 1) - me_d * 4
    starts = jnp.zeros((1, RESP), I32)
    ends = jnp.zeros((1, RESP), I32)
    counts = jnp.ones((1, RESP), I32)
    begin = 0
    for k in range(4):
        starts = jnp.where(lane == k, begin, starts)
        begin = begin + lens[k]
        ends = jnp.where(lane == k, begin, ends)
        counts = jnp.where(lane == k, lens[k], counts)
    mask = ((position >= starts) & (position < ends)).astype(F32)
    inverse = 1.0 / counts.astype(F32)

    top = lax.broadcasted_iota(I32, (8, RESP), 0)
    part = [jnp.sum(mask * (scale[r] * yh[r]), axis=0, keepdims=True) * inverse for r in range(2)]
    tile = jnp.where(top == 0, part[0], jnp.where(top == 1, part[1], 0.0))

    rs1[yc] = tile
    sends1 = []
    for d in range(1, NY * NC):
        other = lax.rem(yc + d, NY * NC)
        copy = remote(rs1.at[yc], rs1.at[yc], r1s.at[d], r1r.at[yc], dev(x, z, other))
        copy.start()
        sends1.append(copy)
    for d in range(1, NY * NC):
        other = lax.rem(yc + d, NY * NC)
        remote(rs1.at[other], rs1.at[other], r1s.at[d], r1r.at[other], dev(x, z, other)).wait_recv()
    rs2[z] = jnp.sum(rs1[...], axis=0)
    sends2 = []
    for d in range(1, NZ):
        other = lax.rem(z + d, NZ)
        copy = remote(rs2.at[z], rs2.at[z], r2s.at[d], r2r.at[z], dev(x, other, yc))
        copy.start()
        sends2.append(copy)
    for d in range(1, NZ):
        other = lax.rem(z + d, NZ)
        remote(rs2.at[other], rs2.at[other], r2s.at[d], r2r.at[other], dev(x, other, yc)).wait_recv()
    mine = jnp.sum(rs2[pl.ds(zh * NZL, NZL)], axis=0)
    theirs = jnp.sum(rs2[pl.ds((1 - zh) * NZL, NZL)], axis=0)
    rewards = mine + jnp.where(top == 0, theirs[1:2], jnp.where(top == 1, theirs[0:1], 0.0))

    order = pv[0:1, :]
    onehot = (lax.broadcasted_iota(I32, (RESP, RESP), 0) == order).astype(F32)
    ordered = dot(rewards, onehot, precision=HIGH)
    even = lax.rem(lax.broadcasted_iota(I32, (8, RESP), 1), 2) == 0
    margin = jnp.where(
        even, ordered - pltpu.roll(ordered, RESP - 1, 1), pltpu.roll(ordered, 1, 1) - ordered
    )
    soft = jnp.log1p(jnp.exp(-jnp.abs(margin))) + jnp.maximum(-margin, 0.0)
    loss_ref[0] = jnp.sum(jnp.where(even & (top == 0), soft, 0.0)) * (2.0 / RESP)
    slope = 1.0 / (1.0 + jnp.exp(margin))
    coef = jnp.where(even, -slope, slope)
    dreward = dot(coef, onehot, NT, precision=HIGH)

    vrows, crows = [], []
    for r in range(2):
        half = slice(r * RANK, (r + 1) * RANK)
        s = scale[r]
        dscore = jnp.sum(mask * (dreward[r : r + 1] * inverse), axis=1, keepdims=True)
        sd = s * dscore
        cc = s * s * s * (dscore * yh[r] * (1.0 / WB))
        qa[:, half] = (sd * uh[:, half] - cc * yu[:, half]).astype(BF16)
        crow = -cc * lowf[:, half]
        crows.append(crow)
        qb[0:ROWS, half] = crow.astype(BF16)
        vrows.append(jnp.sum(sd * lowf[:, half], axis=0, keepdims=True))
    arow2 = lax.broadcasted_iota(I32, (AUG, RANK), 0)
    for r in range(2):
        hi, lo = split(vrows[r])
        tile = jnp.where((arow2 == 3 * r) | (arow2 == 3 * r + 2), hi.astype(F32), 0.0)
        tile = jnp.where(arow2 == 3 * r + 1, lo.astype(F32), tile)
        qb[ROWS : ROWS + AUG, r * RANK : (r + 1) * RANK] = tile.astype(BF16)
    mbd[...] = jnp.where(same, dot(low, qb[0:ROWS, :], TN), 0.0).astype(BF16)

    def feature_chunk(k):
        return lax.rem(zl + 1 + k, NZL)

    def c1copy(k):
        return remote(gr.at[k], rc.at[k], c1s.at[k], c1r.at[k], core_peer)

    def spread(k, tmp, n, rows):
        for d in range(NY):
            own = tmp[pl.ds(pl.multiple_of((2 * d + c) * n, 16), n), :]
            other = tmp[pl.ds(pl.multiple_of((2 * d + 1 - c) * n, 16), n), :].astype(BF16)
            for r in range(2):
                g32[k, r, d, rows, :] = own[:, r * RANK : (r + 1) * RANK]
                gr[k, r, d, rows, :] = other[:, r * RANK : (r + 1) * RANK]

    def terms(k, carry):
        j = feature_chunk(k)
        for i in range(4):
            cols = pl.ds(pl.multiple_of(j * 1024 + i * 256, 256), 256)
            tmpa[i * 256 : (i + 1) * 256, :] = dot(xa[:, cols], qa[...], TN)
        spread(k, tmpa, RA, slice(0, RA))
        for i in range(3):
            first = j * 1152 + i * 384
            cols = pl.ds(pl.multiple_of(first, 128), 384)
            tmpb[i * 384 : (i + 1) * 384, :] = dot(xb[:, cols], qb[...], TN) + dot(
                wcat(WA + first, 384), mbd[...]
            )
        spread(k, tmpb, RB, slice(RA, RAB))
        c1copy(k).start()
        return carry

    lax.fori_loop(0, NZL, terms, 0)

    ya = y + 1 - 2 * lax.rem(y, 2)
    yb = 3 - y
    cut = (slice(0, RA), slice(RA, RAB))

    def flip(v):
        return v + 1 - 2 * lax.rem(v, 2)

    def sent1(p, i):
        to = (ya, yb)[p]
        return to if i == 0 else ((3 - to) if p == 0 else flip(to))

    def ycopy1(k, p, i):
        dst = (s2a, s2b)[p].at[k, i]
        return remote(
            b1.at[k, :, i, pl.ds(*((0, RA), (RA, RB))[p])],
            dst, y1s.at[k, p, i], y1r.at[k, p, i], dev(x, z, (ya, yb)[p] * NC + c),
        )

    def ycopy2(k, p):
        to = (yb, ya)[p]
        buf = (sa, sb)[p]
        return remote(
            buf.at[0, k], buf.at[1, k], y2s.at[k, p], y2r.at[k, p], dev(x, z, to * NC + c)
        )

    def fcopy(k, r):
        zt = (zh if r == 0 else 1 - zh) * NZL + feature_chunk(k)
        return remote(b2.at[k, r], fin.at[z], fs.at[k, r], fr.at[z], dev(x, zt, yc))

    def step1(k):
        c1copy(k).wait_recv()
        for i in (1, 0):
            for p in range(2):
                chunk = sent1(p, i)
                total = g32[k, :, chunk, cut[p], :] + rc[k, :, chunk, cut[p], :].astype(F32)
                b1[k, :, i, cut[p], :] = total.astype(BF16)
                ycopy1(k, p, i).start()

    def kept(k, p, chunk, i):
        total = g32[k, :, chunk, cut[p], :] + rc[k, :, chunk, cut[p], :].astype(F32)
        return total + (s2a, s2b)[p][k, i].astype(F32)

    def step2(k):
        for p in range(2):
            ycopy1(k, p, 1).wait_recv()
            (sa, sb)[p][0, k] = kept(k, p, (yb, ya)[p], 1).astype(BF16)
            ycopy2(k, p).start()

    def step3(k):
        for p in range(2):
            ycopy1(k, p, 0).wait_recv()
            ycopy2(k, p).wait_recv()
            total = kept(k, p, y, 0) + (sa, sb)[p][1, k].astype(F32)
            b2[k, :, cut[p], :] = total.astype(BF16)
        for r in range(2):
            if k == NZL - 1 and r == 0:
                fin[z] = b2[k, 0]
            else:
                fcopy(k, r).start()

    step1(0)
    step1(1)
    step2(0)
    step1(2)
    step2(1)
    step3(0)
    step1(3)
    step2(2)
    step3(1)
    step2(3)
    step3(2)
    step3(3)
    for d in range(1, NZ):
        other = lax.rem(z + d, NZ)
        remote(b2.at[0, 0], fin.at[other], fs.at[0, 0], fr.at[other], dev(x, other, yc)).wait_recv()
    total = fin[0].astype(F32)
    for i in range(1, NZ):
        total = total + fin[i].astype(F32)
    ga_ref[0] = total[0:RA]
    gb_ref[0] = total[RA:RAB]

    hcopy.wait_send()
    for i in range(2 * XCH):
        for way in range(3):
            xcopy(i, way).wait_send()

    def zdone(i, carry):
        for s in range(2):
            zcopy(s, i, False).wait_send()
            ccopy(s, i, c).wait_send()
        return carry

    lax.fori_loop(0, ZCH, zdone, 0)
    for copy in sends1 + sends2:
        copy.wait_send()
    for k in range(NZL):
        c1copy(k).wait_send()
        for p in range(2):
            for i in range(2):
                ycopy1(k, p, i).wait_send()
            ycopy2(k, p).wait_send()
        for r in range(2):
            if not (k == NZL - 1 and r == 0):
                fcopy(k, r).wait_send()


def per_device(acts, base, down_matrices, up_matrices, head, gain, lengths, pairing):
    hbm = pl.BlockSpec(memory_space=pltpu.HBM)
    vmem = pl.BlockSpec(memory_space=pltpu.VMEM)
    smem = pl.BlockSpec(memory_space=pltpu.SMEM)
    dma = pltpu.SemaphoreType.DMA
    loss, grad_a, grad_b = pl.pallas_call(
        kernel,
        out_shape=(
            jax.ShapeDtypeStruct((1,), F32),
            jax.ShapeDtypeStruct((1, RA, RANK), F32),
            jax.ShapeDtypeStruct((1, RB, RANK), F32),
        ),
        in_specs=[hbm] * 8,
        out_specs=(smem, vmem, vmem),
        scratch_shapes=[
            pltpu.VMEM((ROWS, WA), BF16),
            pltpu.VMEM((ROWS + AUG, WB), BF16),
            pltpu.VMEM((2, WAB, RANK), BF16),
            pltpu.VMEM((1, WB), BF16),
            pltpu.VMEM((WB // 128, 128), F32),
            pltpu.SMEM((1, 4), I32),
            pltpu.VMEM((1, RESP), I32),
            pltpu.VMEM((40, 128), F32),
            pltpu.VMEM((40, 128), F32),
            pltpu.VMEM((ROWS, 2 * RANK), F32),
            pltpu.VMEM((ROWS, 2 * RANK), F32),
            pltpu.VMEM((ROWS, AUG), F32),
            pltpu.VMEM((ROWS, 128), F32),
            pltpu.VMEM((2 * RANK, 2 * RANK), F32),
            pltpu.VMEM((NY * NC, 8, RESP), F32),
            pltpu.VMEM((NZ, 8, RESP), F32),
            pltpu.VMEM((ROWS, 2 * RANK), BF16),
            pltpu.VMEM((ROWS + AUG, 2 * RANK), BF16),
            pltpu.VMEM((2 * RANK, 2 * RANK), BF16),
            pltpu.VMEM((WA // NZL, 2 * RANK), F32),
            pltpu.VMEM((WB // NZL, 2 * RANK), F32),
            pltpu.VMEM((NZL, 2, NY, RAB, RANK), F32),
            pltpu.VMEM((NZL, 2, NY, RAB, RANK), BF16),
            pltpu.VMEM((NZL, 2, NY, RAB, RANK), BF16),
            pltpu.VMEM((NZL, 2, 2, RAB, RANK), BF16),
            pltpu.VMEM((NZL, 2, 2, RA, RANK), BF16),
            pltpu.VMEM((NZL, 2, 2, RB, RANK), BF16),
            pltpu.VMEM((2, NZL, 2, RA, RANK), BF16),
            pltpu.VMEM((2, NZL, 2, RB, RANK), BF16),
            pltpu.VMEM((NZL, 2, RAB, RANK), BF16),
            pltpu.VMEM((NZ, RAB, RANK), BF16),
            dma((8,)),
            dma((3, 2 * XCH)),
            dma((3, 2 * XCH)),
            dma((2, ZCH)),
            dma((2, ZCH)),
            dma((2, ZCH)),
            dma((2, ZCH)),
            dma,
            dma,
            dma((NY * NC,)),
            dma((NY * NC,)),
            dma((NZ,)),
            dma((NZ,)),
            dma((NZL,)),
            dma((NZL,)),
            dma((NZL, 2, 2)),
            dma((NZL, 2, 2)),
            dma((NZL, 2)),
            dma((NZL, 2)),
            dma((NZL, 2)),
            dma((NZ,)),
        ],
        compiler_params=pltpu.CompilerParams(
            collective_id=0, has_side_effects=True, vmem_limit_bytes=60 * 1024 * 1024
        ),
    )(
        acts, base, down_matrices, up_matrices, head,
        gain.reshape(WB // 128, 128), lengths, pairing.reshape(1, RESP),
    )
    return loss, grad_a, grad_b


def solution(mesh):
    return jax.shard_map(
        per_device,
        mesh=mesh,
        in_specs=(
            P("dp", "member", None, None),
            P("dp", "member", None, None),
            P("member", None, None),
            P("member", None, None),
            P("member", None),
            P(),
            P("dp", None),
            P(),
        ),
        out_specs=(P("member"), P("member", "dp", None), P("member", "dp", None)),
        check_vma=False,
    )
```

time: 592 us -> 106 us (0.18)
  the two profiles are of different devices: /device:TPU:1 before, /device:TPU:2 now
where the time goes in v1:
time: 106 us
  Pallas kernels  101 us (95%)
  local copies, waits for them, and re-layouts  2.99 us (3%)
  between operations  2.39 us (2%)
    pallas_call x1, Pallas kernels, per_device(): pl.pallas_call(kernel, out_shape=(jax.ShapeDtypeStruct((1,), F32), jax.Sh...  101 us
    unnamed x2, local copies, waits for them, and re-layouts  2.99 us

profile of v1, /device:TPU:2, one launch (start us, length us, event | category | flops | bytes accessed | tf_op | source)
XLA Modules:
  0.0 106.0 jit_solution(3524676852790788173)
XLA Ops:
  0.6 100.6 %shard_map.103 = (f32[1]{0:T(128)}, f32[1,128,128]{2,1,0:T(8,128)}, f32[1,144,128]{2,1,0:T(8,128)}) custom-call(bf16[1,1,48,4096]{3,2,1,0:T(8,128)(2,1)} %acts.1, bf16[1,1,48,4608]{3,2,1,0:T(8,128)(2,1)} %base.1, bf16[1,4096,128]{2,1,0:T(8,128)(2,1)} %down.1, bf16[1,4608,128]{2,1,0:T(8,128)(2,1)} %up.1, bf16[1,4608]{1,0:T(2,128)(2,1)} %head.1, ...), custom_call_target="tpu_custom_call" | custom-call | tf_op jit(solution)/shard_map/pallas_call | solution.py:500
  101.9 1.5 %copy.15 = f32[1,128,128]{2,1,0:T(8,128)} copy(f32[1,128,128]{2,1,0:T(8,128)} %get-tuple-element.7) | data formatting | bytes 131072
  103.3 1.5 %copy.16 = f32[1,144,128]{2,1,0:T(8,128)} copy(f32[1,144,128]{2,1,0:T(8,128)} %get-tuple-element.8) | data formatting | bytes 147456

commit v2 on v1

--- a/solution.py
+++ b/solution.py
@@ -7,7 +7,6 @@
 
 F32, BF16, I32 = jnp.float32, jnp.bfloat16, jnp.int32
 MESH = pl.DeviceIdType.MESH
-HIGH = lax.Precision.HIGHEST
 
 NX, NZH, NZL, NY, NC = 4, 2, 4, 4, 2
 NZ = NZH * NZL
@@ -20,15 +19,14 @@
 RESP = 128
 XCH = 2
 WAB = WA + WB
-ZCH = 8
-ZROWS = WAB // 4 // ZCH
-ZLAG = NZL - 1
+WCH = 4
+OFFSETS = (0, 1, 3, 2)
 TN = (((0,), (0,)), ((), ()))
 NT = (((1,), (1,)), ((), ()))
 
 
-def dot(a, b, dims=(((1,), (0,)), ((), ())), precision=None):
-    return lax.dot_general(a, b, dims, precision=precision, preferred_element_type=F32)
+def dot(a, b, dims=(((1,), (0,)), ((), ()))):
+    return lax.dot_general(a, b, dims, preferred_element_type=F32)
 
 
 def split(v):
@@ -36,12 +34,20 @@
     return hi, (v - hi.astype(F32)).astype(BF16)
 
 
+def dot3(v, b, dims=(((1,), (0,)), ((), ()))):
+    hi = v.astype(BF16)
+    rest = v - hi.astype(F32)
+    mid = rest.astype(BF16)
+    low = (rest - mid.astype(F32)).astype(BF16)
+    return dot(hi, b, dims) + dot(mid, b, dims) + dot(low, b, dims)
+
+
 def kernel(
     acts, base, down, up, head, gain, lengths, pairing,
     loss_ref, ga_ref, gb_ref,
-    xa, xb, wv, hv, gv, lv, pv, hpk, hrecv, plow, pt, pbh, pnb, gram, rs1, rs2,
-    qa, qb, mbd, tmpa, tmpb, g32, gr, rc, b1, s2a, s2b, sa, sb, b2, fin,
-    loc, xs, xr, zs, zr, cs, cr, hs, hr, r1s, r1r, r2s, r2r,
+    xa, xb, wv, hv, gv, lv, pv, hpk, hrecv, gram, maskv, apre, cpre, vpre, rs1, rs2,
+    lows, qa, qb, mbd, tmpa, tmpb, g32, gr, rc, b1, s2a, s2b, sa, sb, b2, fin,
+    loc, xs, xr, zs, zr, ws, wr, cs, cr, hs, hr, r1s, r1r, r2s, r2r,
     c1s, c1r, y1s, y1r, y2s, y2r, fs, fr,
 ):
     me_m, me_d = lax.axis_index("member"), lax.axis_index("dp")
@@ -60,7 +66,7 @@
         )
 
     right, left = lax.rem(x + 1, NX), lax.rem(x + 3, NX)
-    zup, zdown, zother = lax.rem(z + 1, NZ), lax.rem(z + 7, NZ), lax.rem(z + 4, NZ)
+    zother = lax.rem(z + NZL, NZ)
     core_peer = dev(x, z, y * NC + 1 - c)
 
     def load(i):
@@ -104,175 +110,42 @@
     def xwait(i, way):
         xcopy(i, way).wait_recv()
 
-    def zrows(s, i, core):
-        return pl.ds(pl.multiple_of((2 * s + core) * (WAB // 4) + i * ZROWS, 16), ZROWS)
-
-    def zcopy(s, i, own):
-        rows = zrows(s, i, c)
-        to = zup if s == 0 else zdown
-        return remote(wv.at[0 if own else 1, rows], wv.at[1, rows], zs.at[s, i], zr.at[s, i], dev(x, to, yc))
-
-    def ccopy(s, i, core):
-        rows = zrows(s, i, core)
-        return remote(wv.at[1, rows], wv.at[1, rows], cs.at[s, i], cr.at[s, i], core_peer)
+    def wpiece(i, eighth):
+        n = (WA if i < WCH // 2 else WB) // (NY * NC) // (WCH // 2)
+        first = eighth * (2 * n) + (i % (WCH // 2)) * n
+        return pl.multiple_of(first, 16), n
+
+    def wrows(i, eighth):
+        first, n = wpiece(i, eighth)
+        return wv.at[1, pl.ds(first + (0 if i < WCH // 2 else WA), n)]
+
+    def zcopy(i):
+        src = (down if i < WCH // 2 else up).at[0, pl.ds(*wpiece(i, yc))]
+        return remote(src, wrows(i, yc), zs.at[i], zr.at[i], dev(x, zother, yc))
+
+    def wcopy(i, d):
+        to = lax.rem(y + d, NY)
+        return remote(wrows(i, yc), wrows(i, yc), ws.at[d, i], wr.at[d, i], dev(x, z, to * NC + c))
+
+    def wfrom(d, core):
+        return lax.rem(y + NY - d, NY) * NC + core
+
+    def ccopy(i, d, core):
+        rows = wrows(i, wfrom(d, core))
+        return remote(rows, rows, cs.at[d, i], cr.at[d, i], core_peer)
 
     for i in range(2 * XCH):
         xcopy(i, 0).start()
         xcopy(i, 1).start()
+        zcopy(i).start()
     load(0).wait()
     for i in range(WB // 128):
         hpk[i : i + 1, :] = hv[0:1, i * 128 : (i + 1) * 128].astype(F32)
     hcopy = remote(hpk, hrecv, hs, hr, dev(x, zother, yc))
     hcopy.start()
-    load(6).wait()
-    load(7).wait()
-    edge = (NZL - 1, 0)
-    for s in range(2):
-        @pl.when(zl == edge[s])
-        def _():
-            for i in range(ZCH):
-                zcopy(s, i, True).start()
-
-    lag = (jnp.maximum(2 * zl - 3, 0), jnp.maximum(3 - 2 * zl, 0))
-
-    def zstep(t, carry):
-        for s in range(2):
-            i = t - lag[s]
-
-            @pl.when((i >= 0) & (i < ZCH))
-            def _():
-                zcopy(s, i, False).wait_recv()
-
-                @pl.when(zl != edge[s])
-                def _():
-                    zcopy(s, i, False).start()
-
-                ccopy(s, i, c).start()
-
-        return carry
-
-    done = 0
-    for i in range(2 * XCH):
-        until = (5, 7, 9, ZCH + ZLAG)[i]
-        lax.fori_loop(done, until, zstep, 0)
-        done = until
-
-        @pl.when(c == 0)
-        def _():
-            xwait(i, 0)
-
-        @pl.when(c == 1)
-        def _():
-            xwait(i, 1)
-
-        xcopy(i, 2).start()
-
-    hcopy.wait_recv()
-    load(1).wait()
-    arow = lax.broadcasted_iota(I32, (AUG, 128), 0)
-    for i in range(WB // 128):
-        cols = slice(i * 128, (i + 1) * 128)
-        g = gv[i : i + 1, :]
-        hi0, lo0 = split(hpk[i : i + 1, :] * g)
-        hi1, lo1 = split(hrecv[i : i + 1, :] * g)
-        tile = jnp.where(arow < 2, hi0.astype(F32), 0.0)
-        tile = jnp.where(arow == 2, lo0.astype(F32), tile)
-        tile = jnp.where((arow == 3) | (arow == 4), hi1.astype(F32), tile)
-        tile = jnp.where(arow == 5, lo1.astype(F32), tile)
-        xb[ROWS : ROWS + AUG, cols] = tile.astype(BF16)
-
-    for i in (2, 3, 4, 5):
-        load(i).wait()
-
-    def cwait(i, carry):
-        for s in range(2):
-            ccopy(s, i, 1 - c).wait_recv()
-        return carry
-
-    lax.fori_loop(0, ZCH, cwait, 0)
-
-    kb = 512
-    gram[...] = jnp.zeros_like(gram)
-
-    def wcat(first, n):
-        rows = pl.ds(pl.multiple_of(first, 16), n)
-        return jnp.concatenate([wv[0, rows, :], wv[1, rows, :]], axis=1)
-
-    def gram_step(i, uh):
-        rows = pl.ds(pl.multiple_of(i * kb, kb), kb)
-        u = wcat(WA + i * kb, kb)
-        gram[...] += dot(u, u, TN)
-        return uh + dot(xb[pl.ds(ROWS, AUG), rows], u)
-
-    uh16 = lax.fori_loop(0, WB // kb, gram_step, jnp.zeros((AUG, 2 * RANK), F32))
-    lane2 = lax.broadcasted_iota(I32, (1, 2 * RANK), 1)
-    uh = jnp.where(lane2 < RANK, uh16[0:1] + uh16[2:3], uh16[3:4] + uh16[5:6])
-    same = (lax.broadcasted_iota(I32, (2 * RANK, 2 * RANK), 0) < RANK) == (
-        lax.broadcasted_iota(I32, (2 * RANK, 2 * RANK), 1) < RANK
-    )
-    gram_hi, gram_lo = split(jnp.where(same, gram[...], 0.0))
-
-    def forward(first, n):
-        rows = pl.ds(first, n)
-
-        def step_a(i, acc):
-            k = pl.ds(pl.multiple_of(i * kb, kb), kb)
-            return acc + dot(xa[rows, k], wcat(i * kb, kb))
-
-        plow[rows, :] = lax.fori_loop(0, WA // kb, step_a, jnp.zeros((n, 2 * RANK), F32))
-
-        def step_b(i, acc):
-            t, bh, nb = acc
-            k = pl.ds(pl.multiple_of(i * kb, kb), kb)
-            block = xb[rows, k]
-            wide = block.astype(F32)
-            square = wide * wide
-            for j in range(kb // 128):
-                nb = nb + square[:, j * 128 : (j + 1) * 128]
-            return (t + dot(block, wcat(WA + i * kb, kb)), bh + dot(block, xb[pl.ds(ROWS, AUG), k], NT), nb)
-
-        t, bh, nb = lax.fori_loop(
-            0,
-            WB // kb,
-            step_b,
-            (jnp.zeros((n, 2 * RANK), F32), jnp.zeros((n, AUG), F32), jnp.zeros((n, 128), F32)),
-        )
-        pt[rows, :] = t
-        pbh[rows, :] = bh
-        pnb[rows, :] = nb
-
-    for i in range(2 * XCH):
-        @pl.when(c == 0)
-        def _():
-            xwait(i, 1)
-
-        @pl.when(c == 1)
-        def _():
-            xwait(i, 0)
-
-    forward(0, 3 * TOK)
-    for i in range(2 * XCH):
-        xwait(i, 2)
-    forward(3 * TOK, TOK)
-
-    low = plow[...].astype(BF16)
-    lowf = low.astype(F32)
-    yu = pt[...] + dot(low, gram_hi) + dot(low, gram_lo)
-    cross = lowf * (pt[...] + yu)
-    along = lowf * uh
-    nb = jnp.sum(pnb[...], axis=1, keepdims=True)
-    bh = pbh[...]
-    scale, yh = [], []
-    for r in range(2):
-        half = slice(r * RANK, (r + 1) * RANK)
-        n2 = jnp.maximum(nb + jnp.sum(cross[:, half], axis=1, keepdims=True), 0.0)
-        scale.append(lax.rsqrt(n2 * (1.0 / WB) + 1e-06))
-        yh.append(
-            bh[:, 3 * r : 3 * r + 1]
-            + bh[:, 3 * r + 2 : 3 * r + 3]
-            + jnp.sum(along[:, half], axis=1, keepdims=True)
-        )
-
+
+    load(2).wait()
+    load(3).wait()
     row = lax.broadcasted_iota(I32, (ROWS, RESP), 0)
     slot = jnp.where(row < TOK, 0, jnp.where(row < 2 * TOK, 3, jnp.where(row < 3 * TOK, 1, 2)))
     shift = jnp.where(row < TOK, 0, jnp.where(row < 2 * TOK, 1, jnp.where(row < 3 * TOK, 2, 3)))
@@ -290,12 +163,143 @@
         begin = begin + lens[k]
         ends = jnp.where(lane == k, begin, ends)
         counts = jnp.where(lane == k, lens[k], counts)
-    mask = ((position >= starts) & (position < ends)).astype(F32)
     inverse = 1.0 / counts.astype(F32)
+    maskv[...] = jnp.where((position >= starts) & (position < ends), inverse, 0.0)
+    order = jnp.broadcast_to(pv[0:1, :], (8, RESP))
+    even8 = lax.rem(lax.broadcasted_iota(I32, (8, RESP), 1), 2) == 0
+    swapped = jnp.where(even8, pltpu.roll(order, RESP - 1, 1), pltpu.roll(order, 1, 1))
+    number = lax.broadcasted_iota(I32, (RESP, RESP), 0)
+    sign = jnp.where(lax.rem(lax.broadcasted_iota(I32, (1, RESP), 1), 2) == 0, 1.0, -1.0)
+    onehot = jnp.where(number == order[0:1], sign, 0.0)
+    pairs = (onehot - jnp.where(number == swapped[0:1], sign, 0.0)).astype(BF16)
+    onehot = onehot.astype(BF16)
+
+    for i in range(2 * XCH):
+        zcopy(i).wait_recv()
+        for d in range(1, NY):
+            wcopy(i, d).start()
+        ccopy(i, 0, c).start()
+
+        @pl.when(c == 0)
+        def _():
+            xwait(i, 0)
+
+        @pl.when(c == 1)
+        def _():
+            xwait(i, 1)
+
+        xcopy(i, 2).start()
+
+    hcopy.wait_recv()
+    load(1).wait()
+    arow = lax.broadcasted_iota(I32, (AUG, 128), 0)
+    for i in range(WB // 128):
+        cols = slice(i * 128, (i + 1) * 128)
+        g = gv[i : i + 1, :]
+        hi0, lo0 = split(hpk[i : i + 1, :] * g)
+        hi1, lo1 = split(hrecv[i : i + 1, :] * g)
+        tile = jnp.where(arow < 2, hi0.astype(F32), 0.0)
+        tile = jnp.where(arow == 2, lo0.astype(F32), tile)
+        tile = jnp.where((arow == 3) | (arow == 4), hi1.astype(F32), tile)
+        tile = jnp.where(arow == 5, lo1.astype(F32), tile)
+        xb[ROWS : ROWS + AUG, cols] = tile.astype(BF16)
+
+    for i in range(WCH):
+        for d in range(1, NY):
+            remote(
+                wrows(i, wfrom(d, c)), wrows(i, wfrom(d, c)), ws.at[d, i], wr.at[d, i], core_peer
+            ).wait_recv()
+            ccopy(i, d, c).start()
+    for i in (4, 5, 6, 7):
+        load(i).wait()
+    for i in range(WCH):
+        for d in range(NY):
+            ccopy(i, d, 1 - c).wait_recv()
+
+    kb = 512
+    gram[...] = jnp.zeros_like(gram)
+
+    def wcat(first, n):
+        rows = pl.ds(pl.multiple_of(first, 16), n)
+        return jnp.concatenate([wv[0, rows, :], wv[1, rows, :]], axis=1)
+
+    def gram_step(i, uh):
+        rows = pl.ds(pl.multiple_of(i * kb, kb), kb)
+        u = wcat(WA + i * kb, kb)
+        gram[...] += dot(u, u, TN)
+        return uh + dot(xb[pl.ds(ROWS, AUG), rows], u)
+
+    uh16 = lax.fori_loop(0, WB // kb, gram_step, jnp.zeros((AUG, 2 * RANK), F32))
+    lane2 = lax.broadcasted_iota(I32, (1, 2 * RANK), 1)
+    uh = jnp.where(lane2 < RANK, uh16[0:1] + uh16[2:3], uh16[3:4] + uh16[5:6])
+    same = (lax.broadcasted_iota(I32, (2 * RANK, 2 * RANK), 0) < RANK) == (
+        lax.broadcasted_iota(I32, (2 * RANK, 2 * RANK), 1) < RANK
+    )
+    gram_hi, gram_lo = split(jnp.where(same, gram[...], 0.0))
 
     top = lax.broadcasted_iota(I32, (8, RESP), 0)
-    part = [jnp.sum(mask * (scale[r] * yh[r]), axis=0, keepdims=True) * inverse for r in range(2)]
-    tile = jnp.where(top == 0, part[0], jnp.where(top == 1, part[1], 0.0))
+
+    def forward(first, n):
+        rows = pl.ds(first, n)
+
+        def step_a(i, acc):
+            k = pl.ds(pl.multiple_of(i * kb, kb), kb)
+            return acc + dot(xa[rows, k], wcat(i * kb, kb))
+
+        low = lax.fori_loop(0, WA // kb, step_a, jnp.zeros((n, 2 * RANK), F32)).astype(BF16)
+
+        def step_b(i, acc):
+            t, bh, nb = acc
+            k = pl.ds(pl.multiple_of(i * kb, kb), kb)
+            block = xb[rows, k]
+            wide = block.astype(F32)
+            square = wide * wide
+            for j in range(kb // 128):
+                nb = nb + square[:, j * 128 : (j + 1) * 128]
+            return (t + dot(block, wcat(WA + i * kb, kb)), bh + dot(block, xb[pl.ds(ROWS, AUG), k], NT), nb)
+
+        t, bh, nb = lax.fori_loop(
+            0,
+            WB // kb,
+            step_b,
+            (jnp.zeros((n, 2 * RANK), F32), jnp.zeros((n, AUG), F32), jnp.zeros((n, 128), F32)),
+        )
+        lows[rows, :] = low
+        lowf = low.astype(F32)
+        yu = t + dot(low, gram_hi) + dot(low, gram_lo)
+        cross = lowf * (t + yu)
+        along = lowf * uh
+        norm = jnp.sum(nb, axis=1, keepdims=True)
+        rewards = []
+        for r in range(2):
+            half = slice(r * RANK, (r + 1) * RANK)
+            n2 = jnp.maximum(norm + jnp.sum(cross[:, half], axis=1, keepdims=True), 0.0)
+            s = lax.rsqrt(n2 * (1.0 / WB) + 1e-06)
+            yh = (
+                bh[:, 3 * r : 3 * r + 1]
+                + bh[:, 3 * r + 2 : 3 * r + 3]
+                + jnp.sum(along[:, half], axis=1, keepdims=True)
+            )
+            cc = s * s * s * (yh * (1.0 / WB))
+            apre[rows, half] = s * uh[:, half] - cc * yu[:, half]
+            cpre[rows, half] = -cc * lowf[:, half]
+            vpre[rows, half] = s * lowf[:, half]
+            rewards.append(jnp.sum(maskv[rows, :] * (s * yh), axis=0, keepdims=True))
+        return jnp.where(top == 0, rewards[0], jnp.where(top == 1, rewards[1], 0.0))
+
+    for i in range(2 * XCH):
+        @pl.when(c == 0)
+        def _():
+            xwait(i, 1)
+
+        @pl.when(c == 1)
+        def _():
+            xwait(i, 0)
+
+    tile = forward(0, 3 * TOK)
+    for i in range(2 * XCH):
+        xwait(i, 2)
+    tile = tile + forward(3 * TOK, TOK)
 
     rs1[yc] = tile
     sends1 = []
@@ -321,41 +325,26 @@
     theirs = jnp.sum(rs2[pl.ds((1 - zh) * NZL, NZL)], axis=0)
     rewards = mine + jnp.where(top == 0, theirs[1:2], jnp.where(top == 1, theirs[0:1], 0.0))
 
-    order = pv[0:1, :]
-    onehot = (lax.broadcasted_iota(I32, (RESP, RESP), 0) == order).astype(F32)
-    ordered = dot(rewards, onehot, precision=HIGH)
-    even = lax.rem(lax.broadcasted_iota(I32, (8, RESP), 1), 2) == 0
-    margin = jnp.where(
-        even, ordered - pltpu.roll(ordered, RESP - 1, 1), pltpu.roll(ordered, 1, 1) - ordered
-    )
-    soft = jnp.log1p(jnp.exp(-jnp.abs(margin))) + jnp.maximum(-margin, 0.0)
-    loss_ref[0] = jnp.sum(jnp.where(even & (top == 0), soft, 0.0)) * (2.0 / RESP)
+    margin = dot3(rewards, pairs)
     slope = 1.0 / (1.0 + jnp.exp(margin))
-    coef = jnp.where(even, -slope, slope)
-    dreward = dot(coef, onehot, NT, precision=HIGH)
-
-    vrows, crows = [], []
+    dreward = -dot3(slope, onehot, NT)
+    vrows = []
     for r in range(2):
         half = slice(r * RANK, (r + 1) * RANK)
-        s = scale[r]
-        dscore = jnp.sum(mask * (dreward[r : r + 1] * inverse), axis=1, keepdims=True)
-        sd = s * dscore
-        cc = s * s * s * (dscore * yh[r] * (1.0 / WB))
-        qa[:, half] = (sd * uh[:, half] - cc * yu[:, half]).astype(BF16)
-        crow = -cc * lowf[:, half]
-        crows.append(crow)
-        qb[0:ROWS, half] = crow.astype(BF16)
-        vrows.append(jnp.sum(sd * lowf[:, half], axis=0, keepdims=True))
+        dscore = jnp.sum(maskv[...] * dreward[r : r + 1], axis=1, keepdims=True)
+        qa[:, half] = (dscore * apre[:, half]).astype(BF16)
+        qb[0:ROWS, half] = (dscore * cpre[:, half]).astype(BF16)
+        vrows.append(jnp.sum(dscore * vpre[:, half], axis=0, keepdims=True))
     arow2 = lax.broadcasted_iota(I32, (AUG, RANK), 0)
     for r in range(2):
         hi, lo = split(vrows[r])
         tile = jnp.where((arow2 == 3 * r) | (arow2 == 3 * r + 2), hi.astype(F32), 0.0)
         tile = jnp.where(arow2 == 3 * r + 1, lo.astype(F32), tile)
         qb[ROWS : ROWS + AUG, r * RANK : (r + 1) * RANK] = tile.astype(BF16)
-    mbd[...] = jnp.where(same, dot(low, qb[0:ROWS, :], TN), 0.0).astype(BF16)
+    mbd[...] = jnp.where(same, dot(lows[...], qb[0:ROWS, :], TN), 0.0).astype(BF16)
 
     def feature_chunk(k):
-        return lax.rem(zl + 1 + k, NZL)
+        return lax.rem(zl + OFFSETS[k], NZL)
 
     def c1copy(k):
         return remote(gr.at[k], rc.at[k], c1s.at[k], c1r.at[k], core_peer)
@@ -368,7 +357,7 @@
                 g32[k, r, d, rows, :] = own[:, r * RANK : (r + 1) * RANK]
                 gr[k, r, d, rows, :] = other[:, r * RANK : (r + 1) * RANK]
 
-    def terms(k, carry):
+    def terms(k):
         j = feature_chunk(k)
         for i in range(4):
             cols = pl.ds(pl.multiple_of(j * 1024 + i * 256, 256), 256)
@@ -382,9 +371,6 @@
             )
         spread(k, tmpb, RB, slice(RA, RAB))
         c1copy(k).start()
-        return carry
-
-    lax.fori_loop(0, NZL, terms, 0)
 
     ya = y + 1 - 2 * lax.rem(y, 2)
     yb = 3 - y
@@ -441,18 +427,24 @@
             total = kept(k, p, y, 0) + (sa, sb)[p][1, k].astype(F32)
             b2[k, :, cut[p], :] = total.astype(BF16)
         for r in range(2):
-            if k == NZL - 1 and r == 0:
+            if k == 0 and r == 0:
                 fin[z] = b2[k, 0]
             else:
                 fcopy(k, r).start()
 
+    terms(0)
+    terms(1)
     step1(0)
+    terms(2)
     step1(1)
+    terms(3)
+    step1(2)
     step2(0)
-    step1(2)
+    step1(3)
     step2(1)
     step3(0)
-    step1(3)
+    soft = jnp.log1p(jnp.exp(-jnp.abs(margin))) + jnp.maximum(-margin, 0.0)
+    loss_ref[0] = jnp.sum(jnp.where(even8 & (top == 0), soft, 0.0)) * (2.0 / RESP)
     step2(2)
     step3(1)
     step2(3)
@@ -472,13 +464,12 @@
         for way in range(3):
             xcopy(i, way).wait_send()
 
-    def zdone(i, carry):
-        for s in range(2):
-            zcopy(s, i, False).wait_send()
-            ccopy(s, i, c).wait_send()
-        return carry
-
-    lax.fori_loop(0, ZCH, zdone, 0)
+    for i in range(WCH):
+        zcopy(i).wait_send()
+        for d in range(NY):
+            ccopy(i, d, c).wait_send()
+            if d:
+                wcopy(i, d).wait_send()
     for copy in sends1 + sends2:
         copy.wait_send()
     for k in range(NZL):
@@ -488,7 +479,7 @@
                 ycopy1(k, p, i).wait_send()
             ycopy2(k, p).wait_send()
         for r in range(2):
-            if not (k == NZL - 1 and r == 0):
+            if not (k == 0 and r == 0):
                 fcopy(k, r).wait_send()
 
 
@@ -516,13 +507,14 @@
             pltpu.VMEM((1, RESP), I32),
             pltpu.VMEM((40, 128), F32),
             pltpu.VMEM((40, 128), F32),
+            pltpu.VMEM((2 * RANK, 2 * RANK), F32),
+            pltpu.VMEM((ROWS, RESP), F32),
             pltpu.VMEM((ROWS, 2 * RANK), F32),
             pltpu.VMEM((ROWS, 2 * RANK), F32),
-            pltpu.VMEM((ROWS, AUG), F32),
-            pltpu.VMEM((ROWS, 128), F32),
-            pltpu.VMEM((2 * RANK, 2 * RANK), F32),
+            pltpu.VMEM((ROWS, 2 * RANK), F32),
             pltpu.VMEM((NY * NC, 8, RESP), F32),
             pltpu.VMEM((NZ, 8, RESP), F32),
+            pltpu.VMEM((ROWS, 2 * RANK), BF16),
             pltpu.VMEM((ROWS, 2 * RANK), BF16),
             pltpu.VMEM((ROWS + AUG, 2 * RANK), BF16),
             pltpu.VMEM((2 * RANK, 2 * RANK), BF16),
@@ -541,10 +533,12 @@
             dma((8,)),
             dma((3, 2 * XCH)),
             dma((3, 2 * XCH)),
-            dma((2, ZCH)),
-            dma((2, ZCH)),
-            dma((2, ZCH)),
-            dma((2, ZCH)),
+            dma((WCH,)),
+            dma((WCH,)),
+            dma((NY, WCH)),
+            dma((NY, WCH)),
+            dma((NY, WCH)),
+            dma((NY, WCH)),
             dma,
             dma,
             dma((NY * NC,)),

time: 106 us -> 93 us (0.88)
  the two profiles are of different devices: /device:TPU:2 before, /device:TPU:1 now
where the time goes in v2:
time: 93 us; the launch traced here: 92.8 us
  Pallas kernels  87.4 us (94%)
  local copies, waits for them, and re-layouts  2.99 us (3%)
  between operations  2.39 us (3%)
    pallas_call x1, Pallas kernels, per_device(): pl.pallas_call(kernel, out_shape=(jax.ShapeDtypeStruct((1,), F32), jax.Sh...  87.4 us
    unnamed x2, local copies, waits for them, and re-layouts  2.99 us

profile of v2, /device:TPU:1, one launch (start us, length us, event | category | flops | bytes accessed | tf_op | source)
XLA Modules:
  0.0 92.8 jit_solution(4531350971785742946)
XLA Ops:
  0.6 87.4 %shard_map.103 = (f32[1]{0:T(128)}, f32[1,128,128]{2,1,0:T(8,128)}, f32[1,144,128]{2,1,0:T(8,128)}) custom-call(bf16[1,1,48,4096]{3,2,1,0:T(8,128)(2,1)} %acts.1, bf16[1,1,48,4608]{3,2,1,0:T(8,128)(2,1)} %base.1, bf16[1,4096,128]{2,1,0:T(8,128)(2,1)} %down.1, bf16[1,4608,128]{2,1,0:T(8,128)(2,1)} %up.1, bf16[1,4608]{1,0:T(2,128)(2,1)} %head.1, ...), custom_call_target="tpu_custom_call" | custom-call | tf_op jit(solution)/shard_map/pallas_call | solution.py:491
  88.7 1.5 %copy.15 = f32[1,128,128]{2,1,0:T(8,128)} copy(f32[1,128,128]{2,1,0:T(8,128)} %get-tuple-element.7) | data formatting | bytes 131072
  90.2 1.5 %copy.16 = f32[1,144,128]{2,1,0:T(8,128)} copy(f32[1,144,128]{2,1,0:T(8,128)} %get-tuple-element.8) | data formatting | bytes 147456

commit v3 on v2

--- a/solution.py
+++ b/solution.py
@@ -20,7 +20,9 @@
 XCH = 2
 WAB = WA + WB
 WCH = 4
-OFFSETS = (0, 1, 3, 2)
+OFFSETS = (1, 3, 2, 0)
+UNITS = [(k, r if k < NZL - 1 else 1 - r) for k in range(NZL) for r in range(2)]
+KA, KB = 512, 768
 TN = (((0,), (0,)), ((), ()))
 NT = (((1,), (1,)), ((), ()))
 
@@ -44,7 +46,7 @@
 
 def kernel(
     acts, base, down, up, head, gain, lengths, pairing,
-    loss_ref, ga_ref, gb_ref,
+    loss_ref, out_ref,
     xa, xb, wv, hv, gv, lv, pv, hpk, hrecv, gram, maskv, apre, cpre, vpre, rs1, rs2,
     lows, qa, qb, mbd, tmpa, tmpb, g32, gr, rc, b1, s2a, s2b, sa, sb, b2, fin,
     loc, xs, xr, zs, zr, ws, wr, cs, cr, hs, hr, r1s, r1r, r2s, r2r,
@@ -216,7 +218,6 @@
         for d in range(NY):
             ccopy(i, d, 1 - c).wait_recv()
 
-    kb = 512
     gram[...] = jnp.zeros_like(gram)
 
     def wcat(first, n):
@@ -224,12 +225,12 @@
         return jnp.concatenate([wv[0, rows, :], wv[1, rows, :]], axis=1)
 
     def gram_step(i, uh):
-        rows = pl.ds(pl.multiple_of(i * kb, kb), kb)
-        u = wcat(WA + i * kb, kb)
+        rows = pl.ds(pl.multiple_of(i * KB, KB), KB)
+        u = wcat(WA + i * KB, KB)
         gram[...] += dot(u, u, TN)
         return uh + dot(xb[pl.ds(ROWS, AUG), rows], u)
 
-    uh16 = lax.fori_loop(0, WB // kb, gram_step, jnp.zeros((AUG, 2 * RANK), F32))
+    uh16 = lax.fori_loop(0, WB // KB, gram_step, jnp.zeros((AUG, 2 * RANK), F32))
     lane2 = lax.broadcasted_iota(I32, (1, 2 * RANK), 1)
     uh = jnp.where(lane2 < RANK, uh16[0:1] + uh16[2:3], uh16[3:4] + uh16[5:6])
     same = (lax.broadcasted_iota(I32, (2 * RANK, 2 * RANK), 0) < RANK) == (
@@ -239,31 +240,43 @@
 
     top = lax.broadcasted_iota(I32, (8, RESP), 0)
 
-    def forward(first, n):
+    def forward_a(first, n, begin, end, acc):
         rows = pl.ds(first, n)
 
-        def step_a(i, acc):
-            k = pl.ds(pl.multiple_of(i * kb, kb), kb)
-            return acc + dot(xa[rows, k], wcat(i * kb, kb))
-
-        low = lax.fori_loop(0, WA // kb, step_a, jnp.zeros((n, 2 * RANK), F32)).astype(BF16)
-
-        def step_b(i, acc):
+        def step(i, acc):
+            k = pl.ds(pl.multiple_of(i * KA, KA), KA)
+            return acc + dot(xa[rows, k], wcat(i * KA, KA))
+
+        return lax.fori_loop(begin, end, step, acc)
+
+    def forward_b(first, n, begin, end, acc):
+        rows = pl.ds(first, n)
+
+        def step(i, acc):
             t, bh, nb = acc
-            k = pl.ds(pl.multiple_of(i * kb, kb), kb)
+            k = pl.ds(pl.multiple_of(i * KB, KB), KB)
             block = xb[rows, k]
             wide = block.astype(F32)
             square = wide * wide
-            for j in range(kb // 128):
+            for j in range(KB // 128):
                 nb = nb + square[:, j * 128 : (j + 1) * 128]
-            return (t + dot(block, wcat(WA + i * kb, kb)), bh + dot(block, xb[pl.ds(ROWS, AUG), k], NT), nb)
-
-        t, bh, nb = lax.fori_loop(
-            0,
-            WB // kb,
-            step_b,
-            (jnp.zeros((n, 2 * RANK), F32), jnp.zeros((n, AUG), F32), jnp.zeros((n, 128), F32)),
+            return (
+                t + dot(block, wcat(WA + i * KB, KB)),
+                bh + dot(block, xb[pl.ds(ROWS, AUG), k], NT),
+                nb,
+            )
+
+        return lax.fori_loop(begin, end, step, acc)
+
+    def nothing(n):
+        return jnp.zeros((n, 2 * RANK), F32), (
+            jnp.zeros((n, 2 * RANK), F32), jnp.zeros((n, AUG), F32), jnp.zeros((n, 128), F32),
         )
+
+    def scores(first, n, low32, acc):
+        rows = pl.ds(first, n)
+        low = low32.astype(BF16)
+        t, bh, nb = acc
         lows[rows, :] = low
         lowf = low.astype(F32)
         yu = t + dot(low, gram_hi) + dot(low, gram_lo)
@@ -296,10 +309,19 @@
         def _():
             xwait(i, 0)
 
-    tile = forward(0, 3 * TOK)
-    for i in range(2 * XCH):
+    acc_a, acc_b = nothing(3 * TOK)
+    acc_a = forward_a(0, 3 * TOK, 0, WA // KA, acc_a)
+    acc_b = forward_b(0, 3 * TOK, 0, WB // KB, acc_b)
+    tile = scores(0, 3 * TOK, acc_a, acc_b)
+    acc_a, acc_b = nothing(TOK)
+    na, nb = WA // KA // XCH, WB // KB // XCH
+    for i in range(XCH):
         xwait(i, 2)
-    tile = tile + forward(3 * TOK, TOK)
+        acc_a = forward_a(3 * TOK, TOK, i * na, (i + 1) * na, acc_a)
+    for i in range(XCH):
+        xwait(XCH + i, 2)
+        acc_b = forward_b(3 * TOK, TOK, i * nb, (i + 1) * nb, acc_b)
+    tile = tile + scores(3 * TOK, TOK, acc_a, acc_b)
 
     rs1[yc] = tile
     sends1 = []
@@ -346,8 +368,8 @@
     def feature_chunk(k):
         return lax.rem(zl + OFFSETS[k], NZL)
 
-    def c1copy(k):
-        return remote(gr.at[k], rc.at[k], c1s.at[k], c1r.at[k], core_peer)
+    def c1copy(k, r):
+        return remote(gr.at[k, r], rc.at[k, r], c1s.at[k, r], c1r.at[k, r], core_peer)
 
     def spread(k, tmp, n, rows):
         for d in range(NY):
@@ -370,7 +392,9 @@
                 wcat(WA + first, 384), mbd[...]
             )
         spread(k, tmpb, RB, slice(RA, RAB))
-        c1copy(k).start()
+        for kk, r in UNITS:
+            if kk == k:
+                c1copy(k, r).start()
 
     ya = y + 1 - 2 * lax.rem(y, 2)
     yb = 3 - y
@@ -383,81 +407,76 @@
         to = (ya, yb)[p]
         return to if i == 0 else ((3 - to) if p == 0 else flip(to))
 
-    def ycopy1(k, p, i):
-        dst = (s2a, s2b)[p].at[k, i]
+    def ycopy1(k, r, p, i):
+        u = 2 * k + r
         return remote(
-            b1.at[k, :, i, pl.ds(*((0, RA), (RA, RB))[p])],
-            dst, y1s.at[k, p, i], y1r.at[k, p, i], dev(x, z, (ya, yb)[p] * NC + c),
+            b1.at[k, r, i, pl.ds(*((0, RA), (RA, RB))[p])], (s2a, s2b)[p].at[k, r, i],
+            y1s.at[u, p, i], y1r.at[u, p, i], dev(x, z, (ya, yb)[p] * NC + c),
         )
 
-    def ycopy2(k, p):
-        to = (yb, ya)[p]
+    def ycopy2(k, r, p):
+        u = 2 * k + r
         buf = (sa, sb)[p]
         return remote(
-            buf.at[0, k], buf.at[1, k], y2s.at[k, p], y2r.at[k, p], dev(x, z, to * NC + c)
+            buf.at[0, k, r], buf.at[1, k, r],
+            y2s.at[u, p], y2r.at[u, p], dev(x, z, (yb, ya)[p] * NC + c),
         )
 
     def fcopy(k, r):
         zt = (zh if r == 0 else 1 - zh) * NZL + feature_chunk(k)
         return remote(b2.at[k, r], fin.at[z], fs.at[k, r], fr.at[z], dev(x, zt, yc))
 
-    def step1(k):
-        c1copy(k).wait_recv()
+    def coresum(k, r, p, chunk):
+        return g32[k, r, chunk, cut[p], :] + rc[k, r, chunk, cut[p], :].astype(F32)
+
+    def step1(k, r):
+        c1copy(k, r).wait_recv()
         for i in (1, 0):
             for p in range(2):
-                chunk = sent1(p, i)
-                total = g32[k, :, chunk, cut[p], :] + rc[k, :, chunk, cut[p], :].astype(F32)
-                b1[k, :, i, cut[p], :] = total.astype(BF16)
-                ycopy1(k, p, i).start()
-
-    def kept(k, p, chunk, i):
-        total = g32[k, :, chunk, cut[p], :] + rc[k, :, chunk, cut[p], :].astype(F32)
-        return total + (s2a, s2b)[p][k, i].astype(F32)
-
-    def step2(k):
+                b1[k, r, i, cut[p], :] = coresum(k, r, p, sent1(p, i)).astype(BF16)
+                ycopy1(k, r, p, i).start()
+
+    def kept(k, r, p, chunk, i):
+        return coresum(k, r, p, chunk) + (s2a, s2b)[p][k, r, i].astype(F32)
+
+    def step2(k, r):
         for p in range(2):
-            ycopy1(k, p, 1).wait_recv()
-            (sa, sb)[p][0, k] = kept(k, p, (yb, ya)[p], 1).astype(BF16)
-            ycopy2(k, p).start()
-
-    def step3(k):
+            ycopy1(k, r, p, 1).wait_recv()
+            (sa, sb)[p][0, k, r] = kept(k, r, p, (yb, ya)[p], 1).astype(BF16)
+            ycopy2(k, r, p).start()
+
+    def step3(k, r):
         for p in range(2):
-            ycopy1(k, p, 0).wait_recv()
-            ycopy2(k, p).wait_recv()
-            total = kept(k, p, y, 0) + (sa, sb)[p][1, k].astype(F32)
-            b2[k, :, cut[p], :] = total.astype(BF16)
-        for r in range(2):
-            if k == 0 and r == 0:
-                fin[z] = b2[k, 0]
-            else:
-                fcopy(k, r).start()
+            ycopy1(k, r, p, 0).wait_recv()
+            ycopy2(k, r, p).wait_recv()
+            total = kept(k, r, p, y, 0) + (sa, sb)[p][1, k, r].astype(F32)
+            b2[k, r, cut[p], :] = total.astype(BF16)
+        if (k, r) == UNITS[-1]:
+            fin[z] = b2[k, r]
+        else:
+            fcopy(k, r).start()
 
     terms(0)
     terms(1)
-    step1(0)
-    terms(2)
-    step1(1)
-    terms(3)
-    step1(2)
-    step2(0)
-    step1(3)
-    step2(1)
-    step3(0)
-    soft = jnp.log1p(jnp.exp(-jnp.abs(margin))) + jnp.maximum(-margin, 0.0)
-    loss_ref[0] = jnp.sum(jnp.where(even8 & (top == 0), soft, 0.0)) * (2.0 / RESP)
-    step2(2)
-    step3(1)
-    step2(3)
-    step3(2)
-    step3(3)
+    for u in range(len(UNITS) + 4):
+        if u < len(UNITS):
+            step1(*UNITS[u])
+        if u in (1, 3):
+            terms((u + 3) // 2)
+        if 2 <= u < len(UNITS) + 2:
+            step2(*UNITS[u - 2])
+        if u >= 4:
+            step3(*UNITS[u - 4])
+        if u == len(UNITS) // 2:
+            soft = jnp.log1p(jnp.exp(-jnp.abs(margin))) + jnp.maximum(-margin, 0.0)
+            loss_ref[0] = jnp.sum(jnp.where(even8 & (top == 0), soft, 0.0)) * (2.0 / RESP)
     for d in range(1, NZ):
         other = lax.rem(z + d, NZ)
         remote(b2.at[0, 0], fin.at[other], fs.at[0, 0], fr.at[other], dev(x, other, yc)).wait_recv()
     total = fin[0].astype(F32)
     for i in range(1, NZ):
         total = total + fin[i].astype(F32)
-    ga_ref[0] = total[0:RA]
-    gb_ref[0] = total[RA:RAB]
+    out_ref[...] = total
 
     hcopy.wait_send()
     for i in range(2 * XCH):
@@ -472,15 +491,19 @@
                 wcopy(i, d).wait_send()
     for copy in sends1 + sends2:
         copy.wait_send()
-    for k in range(NZL):
-        c1copy(k).wait_send()
+    for k, r in UNITS:
+        c1copy(k, r).wait_send()
         for p in range(2):
             for i in range(2):
-                ycopy1(k, p, i).wait_send()
-            ycopy2(k, p).wait_send()
-        for r in range(2):
-            if not (k == 0 and r == 0):
-                fcopy(k, r).wait_send()
+                ycopy1(k, r, p, i).wait_send()
+            ycopy2(k, r, p).wait_send()
+        if (k, r) != UNITS[-1]:
+            fcopy(k, r).wait_send()
+
+
+def divide(whole, ga, gb):
+    ga[0] = whole[0:RA]
+    gb[0] = whole[RA:RAB]
 
 
 def per_device(acts, base, down_matrices, up_matrices, head, gain, lengths, pairing):
@@ -488,15 +511,14 @@
     vmem = pl.BlockSpec(memory_space=pltpu.VMEM)
     smem = pl.BlockSpec(memory_space=pltpu.SMEM)
     dma = pltpu.SemaphoreType.DMA
-    loss, grad_a, grad_b = pl.pallas_call(
+    loss, whole = pl.pallas_call(
         kernel,
         out_shape=(
             jax.ShapeDtypeStruct((1,), F32),
-            jax.ShapeDtypeStruct((1, RA, RANK), F32),
-            jax.ShapeDtypeStruct((1, RB, RANK), F32),
+            jax.ShapeDtypeStruct((RAB, RANK), F32),
         ),
         in_specs=[hbm] * 8,
-        out_specs=(smem, vmem, vmem),
+        out_specs=(smem, vmem),
         scratch_shapes=[
             pltpu.VMEM((ROWS, WA), BF16),
             pltpu.VMEM((ROWS + AUG, WB), BF16),
@@ -545,12 +567,12 @@
             dma((NY * NC,)),
             dma((NZ,)),
             dma((NZ,)),
-            dma((NZL,)),
-            dma((NZL,)),
-            dma((NZL, 2, 2)),
-            dma((NZL, 2, 2)),
             dma((NZL, 2)),
             dma((NZL, 2)),
+            dma((2 * NZL, 2, 2)),
+            dma((2 * NZL, 2, 2)),
+            dma((2 * NZL, 2)),
+            dma((2 * NZL, 2)),
             dma((NZL, 2)),
             dma((NZ,)),
         ],
@@ -561,6 +583,15 @@
         acts, base, down_matrices, up_matrices, head,
         gain.reshape(WB // 128, 128), lengths, pairing.reshape(1, RESP),
     )
+    grad_a, grad_b = pl.pallas_call(
+        divide,
+        out_shape=(
+            jax.ShapeDtypeStruct((1, RA, RANK), F32),
+            jax.ShapeDtypeStruct((1, RB, RANK), F32),
+        ),
+        in_specs=[vmem],
+        out_specs=(vmem, vmem),
+    )(whole)
     return loss, grad_a, grad_b
 
 

time: 93 us -> 87.9 us (0.945)
  local copies, waits for them, and re-layouts: 2.99 us -> 0 us
  Pallas kernels: 87.4 us -> 85.4 us
    pallas_call x1, Pallas kernels: 87.4 us -> 83.8 us  [per_device(): pl.pallas_call(kernel, out_shape=(jax.ShapeDtypeStruct((1,), F32), jax.Sh...]
    unnamed x2 -> x0, local copies, waits for them, and re-layouts: 2.99 us -> none
    pallas_call x0 -> x1, Pallas kernels: none -> 1.57 us  [per_device(): pl.pallas_call(divide, out_shape=(jax.ShapeDtypeStruct((1, RA, RANK), F32...]
where the time goes in v3:
time: 87.9 us; the launch traced here: 87.8 us
  Pallas kernels  85.4 us (97%)
  between operations  2.4 us (3%)
    pallas_call x1, Pallas kernels, per_device(): pl.pallas_call(kernel, out_shape=(jax.ShapeDtypeStruct((1,), F32), jax.Sh...  83.8 us

profile of v3, /device:TPU:1, one launch (start us, length us, event | category | flops | bytes accessed | tf_op | source)
XLA Modules:
  0.0 87.8 jit_solution(8419124270223187487)
XLA Ops:
  0.6 83.8 %shard_map.103 = (f32[1]{0:T(128)}, f32[272,128]{1,0:T(8,128)}) custom-call(bf16[1,1,48,4096]{3,2,1,0:T(8,128)(2,1)} %acts.1, bf16[1,1,48,4608]{3,2,1,0:T(8,128)(2,1)} %base.1, bf16[1,4096,128]{2,1,0:T(8,128)(2,1)} %down.1, bf16[1,4608,128]{2,1,0:T(8,128)(2,1)} %up.1, bf16[1,4608]{1,0:T(2,128)(2,1)} %head.1, f32[36,128]{1,0:T(8,128)} %bitcast.2, ...), custom_call_target="tpu_custom_call" | custom-call | tf_op jit(solution)/shard_map/pallas_call | solution.py:514
  84.5 1.6 %shard_map.104 = (f32[1,128,128]{2,1,0:T(8,128)}, f32[1,144,128]{2,1,0:T(8,128)}) custom-call(f32[272,128]{1,0:T(8,128)} %get-tuple-element.8.whole), custom_call_target="tpu_custom_call" | custom-call | tf_op jit(solution)/shard_map/pallas_call | solution.py:586

commit v4 on v3

--- a/solution.py
+++ b/solution.py
@@ -17,11 +17,12 @@
 RA, RB = 128, 144
 RAB = RA + RB
 RESP = 128
-XCH = 2
+XA, XB = 2, 6
+XP = XA + XB
 WAB = WA + WB
 WCH = 4
-OFFSETS = (1, 3, 2, 0)
-UNITS = [(k, r if k < NZL - 1 else 1 - r) for k in range(NZL) for r in range(2)]
+OFFSETS = (0, 3, 1, 2)
+UNITS = ((0, 4), (1, 3), (2, -3), (3, 2), (3, -2), (2, 1), (1, -1), (0, 0))
 KA, KB = 512, 768
 TN = (((0,), (0,)), ((), ()))
 NT = (((1,), (1,)), ((), ()))
@@ -46,7 +47,7 @@
 
 def kernel(
     acts, base, down, up, head, gain, lengths, pairing,
-    loss_ref, out_ref,
+    out_ref,
     xa, xb, wv, hv, gv, lv, pv, hpk, hrecv, gram, maskv, apre, cpre, vpre, rs1, rs2,
     lows, qa, qb, mbd, tmpa, tmpb, g32, gr, rc, b1, s2a, s2b, sa, sb, b2, fin,
     loc, xs, xr, zs, zr, ws, wr, cs, cr, hs, hr, r1s, r1r, r2s, r2r,
@@ -89,28 +90,40 @@
         pl.semaphore_signal(barrier, inc=1, device_id=peer, device_id_type=MESH)
     pl.semaphore_wait(barrier, len(peers))
 
-    ca, cb = WA // XCH, WB // XCH
+    ca, cb = WA // XA, WB // XB
 
     def xpiece(i, slot):
-        if i < XCH:
+        if i < XA:
             return xa.at[pl.ds(slot * TOK, TOK), pl.ds(i * ca, ca)]
-        return xb.at[pl.ds(slot * TOK, TOK), pl.ds((i - XCH) * cb, cb)]
+        return xb.at[pl.ds(slot * TOK, TOK), pl.ds((i - XA) * cb, cb)]
 
     def xsource(i):
-        if i < XCH:
+        if i < XA:
             return acts.at[0, 0, :, pl.ds(i * ca, ca)]
-        return base.at[0, 0, :, pl.ds((i - XCH) * cb, cb)]
+        return base.at[0, 0, :, pl.ds((i - XA) * cb, cb)]
 
     def xcopy(i, way):
         if way == 0:
             return remote(xsource(i), xpiece(i, 1), xs.at[0, i], xr.at[0, i], dev(right, z, yc))
         if way == 1:
             return remote(xsource(i), xpiece(i, 2), xs.at[1, i], xr.at[1, i], dev(left, z, yc))
-        onward = lax.rem(x + 1 + 2 * c, NX)
-        return remote(xpiece(i, 1 + c), xpiece(i, 3), xs.at[2, i], xr.at[2, i], dev(onward, z, yc))
+        turn = c if i < XA else 1 - c
+        onward = lax.rem(x + 1 + 2 * turn, NX)
+        return remote(xpiece(i, 1 + turn), xpiece(i, 3), xs.at[2, i], xr.at[2, i], dev(onward, z, yc))
 
     def xwait(i, way):
         xcopy(i, way).wait_recv()
+
+    def xwait_side(i, onward):
+        first = 0 if (i < XA) == onward else 1
+
+        @pl.when(c == 0)
+        def _():
+            xwait(i, first)
+
+        @pl.when(c == 1)
+        def _():
+            xwait(i, 1 - first)
 
     def wpiece(i, eighth):
         n = (WA if i < WCH // 2 else WB) // (NY * NC) // (WCH // 2)
@@ -136,10 +149,11 @@
         rows = wrows(i, wfrom(d, core))
         return remote(rows, rows, cs.at[d, i], cr.at[d, i], core_peer)
 
-    for i in range(2 * XCH):
+    for i in range(XP):
         xcopy(i, 0).start()
         xcopy(i, 1).start()
-        zcopy(i).start()
+        if i < WCH:
+            zcopy(i).start()
     load(0).wait()
     for i in range(WB // 128):
         hpk[i : i + 1, :] = hv[0:1, i * 128 : (i + 1) * 128].astype(F32)
@@ -176,20 +190,13 @@
     pairs = (onehot - jnp.where(number == swapped[0:1], sign, 0.0)).astype(BF16)
     onehot = onehot.astype(BF16)
 
-    for i in range(2 * XCH):
-        zcopy(i).wait_recv()
-        for d in range(1, NY):
-            wcopy(i, d).start()
-        ccopy(i, 0, c).start()
-
-        @pl.when(c == 0)
-        def _():
-            xwait(i, 0)
-
-        @pl.when(c == 1)
-        def _():
-            xwait(i, 1)
-
+    for i in range(XP):
+        if i < WCH:
+            zcopy(i).wait_recv()
+            for d in range(1, NY):
+                wcopy(i, d).start()
+            ccopy(i, 0, c).start()
+        xwait_side(i, True)
         xcopy(i, 2).start()
 
     hcopy.wait_recv()
@@ -206,23 +213,49 @@
         tile = jnp.where(arow == 5, lo1.astype(F32), tile)
         xb[ROWS : ROWS + AUG, cols] = tile.astype(BF16)
 
-    for i in range(WCH):
-        for d in range(1, NY):
-            remote(
-                wrows(i, wfrom(d, c)), wrows(i, wfrom(d, c)), ws.at[d, i], wr.at[d, i], core_peer
-            ).wait_recv()
-            ccopy(i, d, c).start()
-    for i in (4, 5, 6, 7):
-        load(i).wait()
-    for i in range(WCH):
-        for d in range(NY):
-            ccopy(i, d, 1 - c).wait_recv()
-
-    gram[...] = jnp.zeros_like(gram)
+    def share(pieces):
+        for i in pieces:
+            for d in range(1, NY):
+                remote(
+                    wrows(i, wfrom(d, c)), wrows(i, wfrom(d, c)), ws.at[d, i], wr.at[d, i], core_peer
+                ).wait_recv()
+                ccopy(i, d, c).start()
+
+    def shared(pieces):
+        for i in pieces:
+            for d in range(NY):
+                ccopy(i, d, 1 - c).wait_recv()
 
     def wcat(first, n):
         rows = pl.ds(pl.multiple_of(first, 16), n)
         return jnp.concatenate([wv[0, rows, :], wv[1, rows, :]], axis=1)
+
+    def forward_a(first, n, begin, end, acc):
+        rows = pl.ds(first, n)
+
+        def step(i, acc):
+            k = pl.ds(pl.multiple_of(i * KA, KA), KA)
+            return acc + dot(xa[rows, k], wcat(i * KA, KA))
+
+        return lax.fori_loop(begin, end, step, acc)
+
+    def nothing(n):
+        return jnp.zeros((n, 2 * RANK), F32), (
+            jnp.zeros((n, 2 * RANK), F32), jnp.zeros((n, AUG), F32), jnp.zeros((n, 128), F32),
+        )
+
+    for i in (4, 5, 6, 7):
+        load(i).wait()
+    share(range(WCH // 2))
+    shared(range(WCH // 2))
+    for i in range(XA):
+        xwait_side(i, False)
+    near_a, near_b = nothing(3 * TOK)
+    near_a = forward_a(0, 3 * TOK, 0, WA // KA, near_a)
+    share(range(WCH // 2, WCH))
+    shared(range(WCH // 2, WCH))
+
+    gram[...] = jnp.zeros_like(gram)
 
     def gram_step(i, uh):
         rows = pl.ds(pl.multiple_of(i * KB, KB), KB)
@@ -239,15 +272,6 @@
     gram_hi, gram_lo = split(jnp.where(same, gram[...], 0.0))
 
     top = lax.broadcasted_iota(I32, (8, RESP), 0)
-
-    def forward_a(first, n, begin, end, acc):
-        rows = pl.ds(first, n)
-
-        def step(i, acc):
-            k = pl.ds(pl.multiple_of(i * KA, KA), KA)
-            return acc + dot(xa[rows, k], wcat(i * KA, KA))
-
-        return lax.fori_loop(begin, end, step, acc)
 
     def forward_b(first, n, begin, end, acc):
         rows = pl.ds(first, n)
@@ -268,20 +292,20 @@
 
         return lax.fori_loop(begin, end, step, acc)
 
-    def nothing(n):
-        return jnp.zeros((n, 2 * RANK), F32), (
-            jnp.zeros((n, 2 * RANK), F32), jnp.zeros((n, AUG), F32), jnp.zeros((n, 128), F32),
-        )
-
-    def scores(first, n, low32, acc):
-        rows = pl.ds(first, n)
+    def early(low32, rows):
         low = low32.astype(BF16)
+        lowf = low.astype(F32)
+        lows[rows, :] = low
+        along = lowf * uh
+        return lowf, dot(low, gram_hi) + dot(low, gram_lo), [
+            jnp.sum(along[:, r * RANK : (r + 1) * RANK], axis=1, keepdims=True) for r in range(2)
+        ]
+
+    def scores(rows, before, acc):
+        lowf, lowg, along = before
         t, bh, nb = acc
-        lows[rows, :] = low
-        lowf = low.astype(F32)
-        yu = t + dot(low, gram_hi) + dot(low, gram_lo)
+        yu = t + lowg
         cross = lowf * (t + yu)
-        along = lowf * uh
         norm = jnp.sum(nb, axis=1, keepdims=True)
         rewards = []
         for r in range(2):
@@ -291,7 +315,7 @@
             yh = (
                 bh[:, 3 * r : 3 * r + 1]
                 + bh[:, 3 * r + 2 : 3 * r + 3]
-                + jnp.sum(along[:, half], axis=1, keepdims=True)
+                + along[r]
             )
             cc = s * s * s * (yh * (1.0 / WB))
             apre[rows, half] = s * uh[:, half] - cc * yu[:, half]
@@ -300,28 +324,22 @@
             rewards.append(jnp.sum(maskv[rows, :] * (s * yh), axis=0, keepdims=True))
         return jnp.where(top == 0, rewards[0], jnp.where(top == 1, rewards[1], 0.0))
 
-    for i in range(2 * XCH):
-        @pl.when(c == 0)
-        def _():
-            xwait(i, 1)
-
-        @pl.when(c == 1)
-        def _():
-            xwait(i, 0)
-
-    acc_a, acc_b = nothing(3 * TOK)
-    acc_a = forward_a(0, 3 * TOK, 0, WA // KA, acc_a)
-    acc_b = forward_b(0, 3 * TOK, 0, WB // KB, acc_b)
-    tile = scores(0, 3 * TOK, acc_a, acc_b)
-    acc_a, acc_b = nothing(TOK)
-    na, nb = WA // KA // XCH, WB // KB // XCH
-    for i in range(XCH):
+    for i in range(XA, XP):
+        xwait_side(i, False)
+    near_b = forward_b(0, 3 * TOK, 0, WB // KB, near_b)
+    near = pl.ds(0, 3 * TOK)
+    tile = scores(near, early(near_a, near), near_b)
+    far_a, far_b = nothing(TOK)
+    na, nb = WA // KA // XA, WB // KB // XB
+    for i in range(XA):
         xwait(i, 2)
-        acc_a = forward_a(3 * TOK, TOK, i * na, (i + 1) * na, acc_a)
-    for i in range(XCH):
-        xwait(XCH + i, 2)
-        acc_b = forward_b(3 * TOK, TOK, i * nb, (i + 1) * nb, acc_b)
-    tile = tile + scores(3 * TOK, TOK, acc_a, acc_b)
+        far_a = forward_a(3 * TOK, TOK, i * na, (i + 1) * na, far_a)
+    far = pl.ds(3 * TOK, TOK)
+    before = early(far_a, far)
+    for i in range(XB):
+        xwait(XA + i, 2)
+        far_b = forward_b(3 * TOK, TOK, i * nb, (i + 1) * nb, far_b)
+    tile = tile + scores(far, before, far_b)
 
     rs1[yc] = tile
     sends1 = []
@@ -330,6 +348,17 @@
         copy = remote(rs1.at[yc], rs1.at[yc], r1s.at[d], r1r.at[yc], dev(x, z, other))
         copy.start()
         sends1.append(copy)
+    hcopy.wait_send()
+    for i in range(XP):
+        for way in range(3):
+            xcopy(i, way).wait_send()
+
+    for i in range(WCH):
+        zcopy(i).wait_send()
+        for d in range(NY):
+            ccopy(i, d, c).wait_send()
+            if d:
+                wcopy(i, d).wait_send()
     for d in range(1, NY * NC):
         other = lax.rem(yc + d, NY * NC)
         remote(rs1.at[other], rs1.at[other], r1s.at[d], r1r.at[other], dev(x, z, other)).wait_recv()
@@ -368,8 +397,17 @@
     def feature_chunk(k):
         return lax.rem(zl + OFFSETS[k], NZL)
 
-    def c1copy(k, r):
-        return remote(gr.at[k, r], rc.at[k, r], c1s.at[k, r], c1r.at[k, r], core_peer)
+    def target(u):
+        return lax.rem(z + UNITS[u][1] + NZ, NZ)
+
+    def place_of(u):
+        half = lax.div(target(u), NZL)
+        return UNITS[u][0], jnp.where(half == zh, 0, 1)
+
+    places = [place_of(u) for u in range(len(UNITS))]
+
+    def c1copy(u):
+        return remote(gr.at[places[u]], rc.at[places[u]], c1s.at[u], c1r.at[u], core_peer)
 
     def spread(k, tmp, n, rows):
         for d in range(NY):
@@ -392,9 +430,6 @@
                 wcat(WA + first, 384), mbd[...]
             )
         spread(k, tmpb, RB, slice(RA, RAB))
-        for kk, r in UNITS:
-            if kk == k:
-                c1copy(k, r).start()
 
     ya = y + 1 - 2 * lax.rem(y, 2)
     yb = 3 - y
@@ -407,103 +442,99 @@
         to = (ya, yb)[p]
         return to if i == 0 else ((3 - to) if p == 0 else flip(to))
 
-    def ycopy1(k, r, p, i):
-        u = 2 * k + r
+    def ycopy1(u, p, i):
         return remote(
-            b1.at[k, r, i, pl.ds(*((0, RA), (RA, RB))[p])], (s2a, s2b)[p].at[k, r, i],
+            b1.at[u, i, pl.ds(*((0, RA), (RA, RB))[p])], (s2a, s2b)[p].at[u, i],
             y1s.at[u, p, i], y1r.at[u, p, i], dev(x, z, (ya, yb)[p] * NC + c),
         )
 
-    def ycopy2(k, r, p):
-        u = 2 * k + r
+    def ycopy2(u, p):
         buf = (sa, sb)[p]
         return remote(
-            buf.at[0, k, r], buf.at[1, k, r],
-            y2s.at[u, p], y2r.at[u, p], dev(x, z, (yb, ya)[p] * NC + c),
+            buf.at[0, u], buf.at[1, u], y2s.at[u, p], y2r.at[u, p], dev(x, z, (yb, ya)[p] * NC + c)
         )
 
-    def fcopy(k, r):
-        zt = (zh if r == 0 else 1 - zh) * NZL + feature_chunk(k)
-        return remote(b2.at[k, r], fin.at[z], fs.at[k, r], fr.at[z], dev(x, zt, yc))
-
-    def coresum(k, r, p, chunk):
+    def fcopy(u):
+        return remote(b2.at[u], fin.at[z], fs.at[u], fr.at[z], dev(x, target(u), yc))
+
+    def coresum(u, p, chunk):
+        k, r = places[u]
         return g32[k, r, chunk, cut[p], :] + rc[k, r, chunk, cut[p], :].astype(F32)
 
-    def step1(k, r):
-        c1copy(k, r).wait_recv()
+    def step1(u):
+        c1copy(u).wait_recv()
         for i in (1, 0):
             for p in range(2):
-                b1[k, r, i, cut[p], :] = coresum(k, r, p, sent1(p, i)).astype(BF16)
-                ycopy1(k, r, p, i).start()
-
-    def kept(k, r, p, chunk, i):
-        return coresum(k, r, p, chunk) + (s2a, s2b)[p][k, r, i].astype(F32)
-
-    def step2(k, r):
+                b1[u, i, cut[p], :] = coresum(u, p, sent1(p, i)).astype(BF16)
+                ycopy1(u, p, i).start()
+
+    def kept(u, p, chunk, i):
+        return coresum(u, p, chunk) + (s2a, s2b)[p][u, i].astype(F32)
+
+    def step2(u):
         for p in range(2):
-            ycopy1(k, r, p, 1).wait_recv()
-            (sa, sb)[p][0, k, r] = kept(k, r, p, (yb, ya)[p], 1).astype(BF16)
-            ycopy2(k, r, p).start()
-
-    def step3(k, r):
+            ycopy1(u, p, 1).wait_recv()
+            (sa, sb)[p][0, u] = kept(u, p, (yb, ya)[p], 1).astype(BF16)
+            ycopy2(u, p).start()
+
+    def sent(u):
+        c1copy(u).wait_send()
         for p in range(2):
-            ycopy1(k, r, p, 0).wait_recv()
-            ycopy2(k, r, p).wait_recv()
-            total = kept(k, r, p, y, 0) + (sa, sb)[p][1, k, r].astype(F32)
-            b2[k, r, cut[p], :] = total.astype(BF16)
-        if (k, r) == UNITS[-1]:
-            fin[z] = b2[k, r]
+            for i in range(2):
+                ycopy1(u, p, i).wait_send()
+            ycopy2(u, p).wait_send()
+        if UNITS[u][1] != 0:
+            fcopy(u).wait_send()
+
+    def step3(u):
+        for p in range(2):
+            ycopy1(u, p, 0).wait_recv()
+            ycopy2(u, p).wait_recv()
+            total = kept(u, p, y, 0) + (sa, sb)[p][1, u].astype(F32)
+            b2[u, cut[p], :] = total.astype(BF16)
+        if UNITS[u][1] == 0:
+            fin[z] = b2[u]
         else:
-            fcopy(k, r).start()
+            fcopy(u).start()
 
     terms(0)
-    terms(1)
+    c1copy(0).start()
     for u in range(len(UNITS) + 4):
+        if u + 1 < NZL:
+            terms(u + 1)
+            c1copy(u + 1).start()
+        if u + 1 == NZL - 1:
+            for later in range(NZL, len(UNITS)):
+                c1copy(later).start()
         if u < len(UNITS):
-            step1(*UNITS[u])
-        if u in (1, 3):
-            terms((u + 3) // 2)
+            step1(u)
         if 2 <= u < len(UNITS) + 2:
-            step2(*UNITS[u - 2])
+            step2(u - 2)
         if u >= 4:
-            step3(*UNITS[u - 4])
+            step3(u - 4)
+        if u >= 5:
+            sent(u - 5)
         if u == len(UNITS) // 2:
+            for copy in sends1 + sends2:
+                copy.wait_send()
             soft = jnp.log1p(jnp.exp(-jnp.abs(margin))) + jnp.maximum(-margin, 0.0)
-            loss_ref[0] = jnp.sum(jnp.where(even8 & (top == 0), soft, 0.0)) * (2.0 / RESP)
+            loss = jnp.sum(jnp.where(even8 & (top == 0), soft, 0.0)) * (2.0 / RESP)
     for d in range(1, NZ):
         other = lax.rem(z + d, NZ)
-        remote(b2.at[0, 0], fin.at[other], fs.at[0, 0], fr.at[other], dev(x, other, yc)).wait_recv()
+        remote(b2.at[0], fin.at[other], fs.at[0], fr.at[other], dev(x, other, yc)).wait_recv()
     total = fin[0].astype(F32)
     for i in range(1, NZ):
         total = total + fin[i].astype(F32)
-    out_ref[...] = total
-
-    hcopy.wait_send()
-    for i in range(2 * XCH):
-        for way in range(3):
-            xcopy(i, way).wait_send()
-
-    for i in range(WCH):
-        zcopy(i).wait_send()
-        for d in range(NY):
-            ccopy(i, d, c).wait_send()
-            if d:
-                wcopy(i, d).wait_send()
-    for copy in sends1 + sends2:
-        copy.wait_send()
-    for k, r in UNITS:
-        c1copy(k, r).wait_send()
-        for p in range(2):
-            for i in range(2):
-                ycopy1(k, r, p, i).wait_send()
-            ycopy2(k, r, p).wait_send()
-        if (k, r) != UNITS[-1]:
-            fcopy(k, r).wait_send()
-
-
-def divide(whole, ga, gb):
+    out_ref[0:RAB, :] = total
+    out_ref[RAB : RAB + 8, :] = jnp.full((8, RANK), loss, F32)
+
+    sent(len(UNITS) - 1)
+
+
+def divide(whole, loss, ga, gb):
     ga[0] = whole[0:RA]
     gb[0] = whole[RA:RAB]
+    loss[0] = jnp.max(whole[RAB : RAB + 8])
 
 
 def per_device(acts, base, down_matrices, up_matrices, head, gain, lengths, pairing):
@@ -511,14 +542,11 @@
     vmem = pl.BlockSpec(memory_space=pltpu.VMEM)
     smem = pl.BlockSpec(memory_space=pltpu.SMEM)
     dma = pltpu.SemaphoreType.DMA
-    loss, whole = pl.pallas_call(
+    whole = pl.pallas_call(
         kernel,
-        out_shape=(
-            jax.ShapeDtypeStruct((1,), F32),
-            jax.ShapeDtypeStruct((RAB, RANK), F32),
-        ),
+        out_shape=jax.ShapeDtypeStruct((RAB + 8, RANK), F32),
         in_specs=[hbm] * 8,
-        out_specs=(smem, vmem),
+        out_specs=vmem,
         scratch_shapes=[
             pltpu.VMEM((ROWS, WA), BF16),
             pltpu.VMEM((ROWS + AUG, WB), BF16),
@@ -545,16 +573,16 @@
             pltpu.VMEM((NZL, 2, NY, RAB, RANK), F32),
             pltpu.VMEM((NZL, 2, NY, RAB, RANK), BF16),
             pltpu.VMEM((NZL, 2, NY, RAB, RANK), BF16),
-            pltpu.VMEM((NZL, 2, 2, RAB, RANK), BF16),
-            pltpu.VMEM((NZL, 2, 2, RA, RANK), BF16),
-            pltpu.VMEM((NZL, 2, 2, RB, RANK), BF16),
-            pltpu.VMEM((2, NZL, 2, RA, RANK), BF16),
-            pltpu.VMEM((2, NZL, 2, RB, RANK), BF16),
-            pltpu.VMEM((NZL, 2, RAB, RANK), BF16),
+            pltpu.VMEM((2 * NZL, 2, RAB, RANK), BF16),
+            pltpu.VMEM((2 * NZL, 2, RA, RANK), BF16),
+            pltpu.VMEM((2 * NZL, 2, RB, RANK), BF16),
+            pltpu.VMEM((2, 2 * NZL, RA, RANK), BF16),
+            pltpu.VMEM((2, 2 * NZL, RB, RANK), BF16),
+            pltpu.VMEM((2 * NZL, RAB, RANK), BF16),
             pltpu.VMEM((NZ, RAB, RANK), BF16),
             dma((8,)),
-            dma((3, 2 * XCH)),
-            dma((3, 2 * XCH)),
+            dma((3, XP)),
+            dma((3, XP)),
             dma((WCH,)),
             dma((WCH,)),
             dma((NY, WCH)),
@@ -567,13 +595,13 @@
             dma((NY * NC,)),
             dma((NZ,)),
             dma((NZ,)),
-            dma((NZL, 2)),
-            dma((NZL, 2)),
+            dma((2 * NZL,)),
+            dma((2 * NZL,)),
             dma((2 * NZL, 2, 2)),
             dma((2 * NZL, 2, 2)),
             dma((2 * NZL, 2)),
             dma((2 * NZL, 2)),
-            dma((NZL, 2)),
+            dma((2 * NZL,)),
             dma((NZ,)),
         ],
         compiler_params=pltpu.CompilerParams(
@@ -583,16 +611,16 @@
         acts, base, down_matrices, up_matrices, head,
         gain.reshape(WB // 128, 128), lengths, pairing.reshape(1, RESP),
     )
-    grad_a, grad_b = pl.pallas_call(
+    return pl.pallas_call(
         divide,
         out_shape=(
+            jax.ShapeDtypeStruct((1,), F32),
             jax.ShapeDtypeStruct((1, RA, RANK), F32),
             jax.ShapeDtypeStruct((1, RB, RANK), F32),
         ),
         in_specs=[vmem],
-        out_specs=(vmem, vmem),
+        out_specs=(smem, vmem, vmem),
     )(whole)
-    return loss, grad_a, grad_b
 
 
 def solution(mesh):

time: 87.9 us -> 84.9 us (0.966); the launches traced: 87.8 us -> 83.2 us
  Pallas kernels: 85.4 us -> 82.6 us
  between operations: 2.4 us -> 0.64 us
    pallas_call x2, Pallas kernels: 85.4 us -> 82.6 us  [the longest x1 81 us: per_device(): pl.pallas_call(kernel, out_shape=jax.ShapeDtypeStruct((RAB + 8, RANK), F3...]
where the time goes in v4:
time: 84.9 us; the launch traced here: 83.2 us
  Pallas kernels  82.6 us (97%)
    pallas_call x1, Pallas kernels, per_device(): pl.pallas_call(kernel, out_shape=jax.ShapeDtypeStruct((RAB + 8, RANK), F3...  81 us

profile of v4, /device:TPU:1, one launch (start us, length us, event | category | flops | bytes accessed | tf_op | source)
XLA Modules:
  0.0 83.2 jit_solution(10910562040218393026)
XLA Ops:
  0.6 81.0 %shard_map.103.whole = f32[280,128]{1,0:T(8,128)} custom-call(bf16[1,1,48,4096]{3,2,1,0:T(8,128)(2,1)} %acts.1, bf16[1,1,48,4608]{3,2,1,0:T(8,128)(2,1)} %base.1, bf16[1,4096,128]{2,1,0:T(8,128)(2,1)} %down.1, bf16[1,4608,128]{2,1,0:T(8,128)(2,1)} %up.1, bf16[1,4608]{1,0:T(2,128)(2,1)} %head.1, f32[36,128]{1,0:T(8,128)} %bitcast.2, s32[1,4]{1,0:T(1,128)} %lengths.1, ...), custom_call_target="tpu_custom_call" | custom-call | tf_op jit(solution)/shard_map/pallas_call | solution.py:545
  81.6 1.6 %shard_map.104 = (f32[1]{0:T(128)}, f32[1,128,128]{2,1,0:T(8,128)}, f32[1,144,128]{2,1,0:T(8,128)}) custom-call(f32[280,128]{1,0:T(8,128)} %shard_map.103.whole), custom_call_target="tpu_custom_call" | custom-call | tf_op jit(solution)/shard_map/pallas_call | solution.py:614

commit v5 on v4

--- a/solution.py
+++ b/solution.py
@@ -17,13 +17,13 @@
 RA, RB = 128, 144
 RAB = RA + RB
 RESP = 128
-XA, XB = 2, 6
+XA, XB = 3, 3
 XP = XA + XB
 WAB = WA + WB
 WCH = 4
 OFFSETS = (0, 3, 1, 2)
 UNITS = ((0, 4), (1, 3), (2, -3), (3, 2), (3, -2), (2, 1), (1, -1), (0, 0))
-KA, KB = 512, 768
+KA, KB = 2048, 2304
 TN = (((0,), (0,)), ((), ()))
 NT = (((1,), (1,)), ((), ()))
 
@@ -48,8 +48,8 @@
 def kernel(
     acts, base, down, up, head, gain, lengths, pairing,
     out_ref,
-    xa, xb, wv, hv, gv, lv, pv, hpk, hrecv, gram, maskv, apre, cpre, vpre, rs1, rs2,
-    lows, qa, qb, mbd, tmpa, tmpb, g32, gr, rc, b1, s2a, s2b, sa, sb, b2, fin,
+    xa, xb, wv, hv, gv, lv, pv, hpk, hrecv, maskv, apre, cpre, vpre, rs1, rs2,
+    lows, qa, qb, mbd, tmpa, tmpb, g32, gr, rc, b1a, b1b, s2a, s2b, sa, sb, b2, fin,
     loc, xs, xr, zs, zr, ws, wr, cs, cr, hs, hr, r1s, r1r, r2s, r2r,
     c1s, c1r, y1s, y1r, y2s, y2r, fs, fr,
 ):
@@ -79,34 +79,28 @@
             (down.at[0], wv.at[0, pl.ds(0, WA)]), (up.at[0], wv.at[0, pl.ds(WA, WB)]),
         )[i], loc.at[i])
 
-    for i in range(8):
-        load(i).start()
-
     barrier = pltpu.get_barrier_semaphore()
     peers = [dev(right, z, yc), dev(left, z, yc)]
     peers += [dev(x, lax.rem(z + d, NZ), yc) for d in range(1, NZ)]
     peers += [dev(x, z, lax.rem(yc + d, NY * NC)) for d in range(1, NY * NC)]
     for peer in peers:
         pl.semaphore_signal(barrier, inc=1, device_id=peer, device_id_type=MESH)
+    for i in (4, 5, 0, 2, 3, 1, 6, 7):
+        load(i).start()
     pl.semaphore_wait(barrier, len(peers))
-
-    ca, cb = WA // XA, WB // XB
 
     def xpiece(i, slot):
         if i < XA:
-            return xa.at[pl.ds(slot * TOK, TOK), pl.ds(i * ca, ca)]
-        return xb.at[pl.ds(slot * TOK, TOK), pl.ds((i - XA) * cb, cb)]
-
-    def xsource(i):
-        if i < XA:
-            return acts.at[0, 0, :, pl.ds(i * ca, ca)]
-        return base.at[0, 0, :, pl.ds((i - XA) * cb, cb)]
+            n = TOK // XA
+            return xa.at[pl.ds(slot * TOK + i * n, n)]
+        n = TOK // XB
+        return xb.at[pl.ds(slot * TOK + (i - XA) * n, n)]
 
     def xcopy(i, way):
         if way == 0:
-            return remote(xsource(i), xpiece(i, 1), xs.at[0, i], xr.at[0, i], dev(right, z, yc))
+            return remote(xpiece(i, 0), xpiece(i, 1), xs.at[0, i], xr.at[0, i], dev(right, z, yc))
         if way == 1:
-            return remote(xsource(i), xpiece(i, 2), xs.at[1, i], xr.at[1, i], dev(left, z, yc))
+            return remote(xpiece(i, 0), xpiece(i, 2), xs.at[1, i], xr.at[1, i], dev(left, z, yc))
         turn = c if i < XA else 1 - c
         onward = lax.rem(x + 1 + 2 * turn, NX)
         return remote(xpiece(i, 1 + turn), xpiece(i, 3), xs.at[2, i], xr.at[2, i], dev(onward, z, yc))
@@ -149,11 +143,13 @@
         rows = wrows(i, wfrom(d, core))
         return remote(rows, rows, cs.at[d, i], cr.at[d, i], core_peer)
 
+    load(4).wait()
+    load(5).wait()
     for i in range(XP):
         xcopy(i, 0).start()
         xcopy(i, 1).start()
-        if i < WCH:
-            zcopy(i).start()
+    for i in range(WCH):
+        zcopy(i).start()
     load(0).wait()
     for i in range(WB // 128):
         hpk[i : i + 1, :] = hv[0:1, i * 128 : (i + 1) * 128].astype(F32)
@@ -190,6 +186,17 @@
     pairs = (onehot - jnp.where(number == swapped[0:1], sign, 0.0)).astype(BF16)
     onehot = onehot.astype(BF16)
 
+    def gram_of(r):
+        def step(i, g):
+            u = wv[r, pl.ds(pl.multiple_of(WA + i * KB, 16), KB), :]
+            return g + dot(u, u, TN)
+
+        return split(lax.fori_loop(0, WB // KB, step, jnp.zeros((RANK, RANK), F32)))
+
+    load(6).wait()
+    load(7).wait()
+    grams = [gram_of(0)]
+
     for i in range(XP):
         if i < WCH:
             zcopy(i).wait_recv()
@@ -244,8 +251,6 @@
             jnp.zeros((n, 2 * RANK), F32), jnp.zeros((n, AUG), F32), jnp.zeros((n, 128), F32),
         )
 
-    for i in (4, 5, 6, 7):
-        load(i).wait()
     share(range(WCH // 2))
     shared(range(WCH // 2))
     for i in range(XA):
@@ -253,53 +258,57 @@
     near_a, near_b = nothing(3 * TOK)
     near_a = forward_a(0, 3 * TOK, 0, WA // KA, near_a)
     share(range(WCH // 2, WCH))
+    for i in range(XA, XP):
+        xwait_side(i, False)
+
+    top = lax.broadcasted_iota(I32, (8, RESP), 0)
+
+    def heads(block, k, acc):
+        bh, nb = acc
+        wide = block.astype(F32)
+        square = wide * wide
+        for j in range(KB // 128):
+            nb = nb + square[:, j * 128 : (j + 1) * 128]
+        return bh + dot(block, xb[pl.ds(ROWS, AUG), k], NT), nb
+
+    def near_heads(i, acc):
+        k = pl.ds(pl.multiple_of(i * KB, KB), KB)
+        return heads(xb[0 : 3 * TOK, k], k, acc)
+
+    def near_b_step(i, acc):
+        t, h = acc
+        k = pl.ds(pl.multiple_of(i * KB, KB), KB)
+        u = wcat(WA + i * KB, KB)
+        return t + dot(xb[0 : 3 * TOK, k], u), h + dot(xb[pl.ds(ROWS, AUG), k], u)
+
+    def far_b_step(i, acc):
+        t, *rest = acc
+        k = pl.ds(pl.multiple_of(i * KB, KB), KB)
+        block = xb[pl.ds(3 * TOK, TOK), k]
+        return t + dot(block, wcat(WA + i * KB, KB)), *heads(block, k, rest)
+
+    t, *near_sums = near_b
+    near_sums = lax.fori_loop(0, WB // KB, near_heads, tuple(near_sums))
     shared(range(WCH // 2, WCH))
-
-    gram[...] = jnp.zeros_like(gram)
-
-    def gram_step(i, uh):
-        rows = pl.ds(pl.multiple_of(i * KB, KB), KB)
-        u = wcat(WA + i * KB, KB)
-        gram[...] += dot(u, u, TN)
-        return uh + dot(xb[pl.ds(ROWS, AUG), rows], u)
-
-    uh16 = lax.fori_loop(0, WB // KB, gram_step, jnp.zeros((AUG, 2 * RANK), F32))
+    t, uh16 = lax.fori_loop(0, WB // KB, near_b_step, (t, jnp.zeros((AUG, 2 * RANK), F32)))
+    grams.append(gram_of(1))
     lane2 = lax.broadcasted_iota(I32, (1, 2 * RANK), 1)
     uh = jnp.where(lane2 < RANK, uh16[0:1] + uh16[2:3], uh16[3:4] + uh16[5:6])
     same = (lax.broadcasted_iota(I32, (2 * RANK, 2 * RANK), 0) < RANK) == (
         lax.broadcasted_iota(I32, (2 * RANK, 2 * RANK), 1) < RANK
     )
-    gram_hi, gram_lo = split(jnp.where(same, gram[...], 0.0))
-
-    top = lax.broadcasted_iota(I32, (8, RESP), 0)
-
-    def forward_b(first, n, begin, end, acc):
-        rows = pl.ds(first, n)
-
-        def step(i, acc):
-            t, bh, nb = acc
-            k = pl.ds(pl.multiple_of(i * KB, KB), KB)
-            block = xb[rows, k]
-            wide = block.astype(F32)
-            square = wide * wide
-            for j in range(KB // 128):
-                nb = nb + square[:, j * 128 : (j + 1) * 128]
-            return (
-                t + dot(block, wcat(WA + i * KB, KB)),
-                bh + dot(block, xb[pl.ds(ROWS, AUG), k], NT),
-                nb,
-            )
-
-        return lax.fori_loop(begin, end, step, acc)
 
     def early(low32, rows):
         low = low32.astype(BF16)
         lowf = low.astype(F32)
         lows[rows, :] = low
         along = lowf * uh
-        return lowf, dot(low, gram_hi) + dot(low, gram_lo), [
-            jnp.sum(along[:, r * RANK : (r + 1) * RANK], axis=1, keepdims=True) for r in range(2)
-        ]
+        lowg, sums = [], []
+        for r, (hi, lo) in enumerate(grams):
+            half = slice(r * RANK, (r + 1) * RANK)
+            lowg.append(dot(low[:, half], hi) + dot(low[:, half], lo))
+            sums.append(jnp.sum(along[:, half], axis=1, keepdims=True))
+        return lowf, jnp.concatenate(lowg, axis=1), sums
 
     def scores(rows, before, acc):
         lowf, lowg, along = before
@@ -324,21 +333,17 @@
             rewards.append(jnp.sum(maskv[rows, :] * (s * yh), axis=0, keepdims=True))
         return jnp.where(top == 0, rewards[0], jnp.where(top == 1, rewards[1], 0.0))
 
-    for i in range(XA, XP):
-        xwait_side(i, False)
-    near_b = forward_b(0, 3 * TOK, 0, WB // KB, near_b)
     near = pl.ds(0, 3 * TOK)
-    tile = scores(near, early(near_a, near), near_b)
+    tile = scores(near, early(near_a, near), (t, *near_sums))
     far_a, far_b = nothing(TOK)
-    na, nb = WA // KA // XA, WB // KB // XB
     for i in range(XA):
         xwait(i, 2)
-        far_a = forward_a(3 * TOK, TOK, i * na, (i + 1) * na, far_a)
+    far_a = forward_a(3 * TOK, TOK, 0, WA // KA, far_a)
     far = pl.ds(3 * TOK, TOK)
     before = early(far_a, far)
     for i in range(XB):
         xwait(XA + i, 2)
-        far_b = forward_b(3 * TOK, TOK, i * nb, (i + 1) * nb, far_b)
+    far_b = lax.fori_loop(0, WB // KB, far_b_step, far_b)
     tile = tile + scores(far, before, far_b)
 
     rs1[yc] = tile
@@ -442,10 +447,10 @@
         to = (ya, yb)[p]
         return to if i == 0 else ((3 - to) if p == 0 else flip(to))
 
-    def ycopy1(u, p, i):
+    def ycopy1(u, p):
         return remote(
-            b1.at[u, i, pl.ds(*((0, RA), (RA, RB))[p])], (s2a, s2b)[p].at[u, i],
-            y1s.at[u, p, i], y1r.at[u, p, i], dev(x, z, (ya, yb)[p] * NC + c),
+            (b1a, b1b)[p].at[u], (s2a, s2b)[p].at[u],
+            y1s.at[u, p], y1r.at[u, p], dev(x, z, (ya, yb)[p] * NC + c),
         )
 
     def ycopy2(u, p):
@@ -463,32 +468,30 @@
 
     def step1(u):
         c1copy(u).wait_recv()
-        for i in (1, 0):
-            for p in range(2):
-                b1[u, i, cut[p], :] = coresum(u, p, sent1(p, i)).astype(BF16)
-                ycopy1(u, p, i).start()
+        for p in range(2):
+            for i in range(2):
+                (b1a, b1b)[p][u, i] = coresum(u, p, sent1(p, i)).astype(BF16)
+            ycopy1(u, p).start()
 
     def kept(u, p, chunk, i):
         return coresum(u, p, chunk) + (s2a, s2b)[p][u, i].astype(F32)
 
     def step2(u):
         for p in range(2):
-            ycopy1(u, p, 1).wait_recv()
+            ycopy1(u, p).wait_recv()
             (sa, sb)[p][0, u] = kept(u, p, (yb, ya)[p], 1).astype(BF16)
             ycopy2(u, p).start()
 
     def sent(u):
         c1copy(u).wait_send()
         for p in range(2):
-            for i in range(2):
-                ycopy1(u, p, i).wait_send()
+            ycopy1(u, p).wait_send()
             ycopy2(u, p).wait_send()
         if UNITS[u][1] != 0:
             fcopy(u).wait_send()
 
     def step3(u):
         for p in range(2):
-            ycopy1(u, p, 0).wait_recv()
             ycopy2(u, p).wait_recv()
             total = kept(u, p, y, 0) + (sa, sb)[p][1, u].astype(F32)
             b2[u, cut[p], :] = total.astype(BF16)
@@ -557,7 +560,6 @@
             pltpu.VMEM((1, RESP), I32),
             pltpu.VMEM((40, 128), F32),
             pltpu.VMEM((40, 128), F32),
-            pltpu.VMEM((2 * RANK, 2 * RANK), F32),
             pltpu.VMEM((ROWS, RESP), F32),
             pltpu.VMEM((ROWS, 2 * RANK), F32),
             pltpu.VMEM((ROWS, 2 * RANK), F32),
@@ -573,7 +575,8 @@
             pltpu.VMEM((NZL, 2, NY, RAB, RANK), F32),
             pltpu.VMEM((NZL, 2, NY, RAB, RANK), BF16),
             pltpu.VMEM((NZL, 2, NY, RAB, RANK), BF16),
-            pltpu.VMEM((2 * NZL, 2, RAB, RANK), BF16),
+            pltpu.VMEM((2 * NZL, 2, RA, RANK), BF16),
+            pltpu.VMEM((2 * NZL, 2, RB, RANK), BF16),
             pltpu.VMEM((2 * NZL, 2, RA, RANK), BF16),
             pltpu.VMEM((2 * NZL, 2, RB, RANK), BF16),
             pltpu.VMEM((2, 2 * NZL, RA, RANK), BF16),
@@ -597,8 +600,8 @@
             dma((NZ,)),
             dma((2 * NZL,)),
             dma((2 * NZL,)),
-            dma((2 * NZL, 2, 2)),
-            dma((2 * NZL, 2, 2)),
+            dma((2 * NZL, 2)),
+            dma((2 * NZL, 2)),
             dma((2 * NZL, 2)),
             dma((2 * NZL, 2)),
             dma((2 * NZL,)),

time: 84.9 us -> 81.2 us (0.956)
  Pallas kernels: 82.6 us -> 79.7 us
    pallas_call x1, Pallas kernels: 81 us -> 78.1 us  [per_device(): pl.pallas_call(kernel, out_shape=jax.ShapeDtypeStruct((RAB + 8, RANK), F3...]
where the time goes in v5:
time: 81.2 us; the launch traced here: 80.4 us
  Pallas kernels  79.7 us (98%)
    pallas_call x1, Pallas kernels, per_device(): pl.pallas_call(kernel, out_shape=jax.ShapeDtypeStruct((RAB + 8, RANK), F3...  78.1 us

profile of v5, /device:TPU:1, one launch (start us, length us, event | category | flops | bytes accessed | tf_op | source)
XLA Modules:
  0.0 80.4 jit_solution(12152082315329683646)
XLA Ops:
  0.6 78.1 %shard_map.103.whole = f32[280,128]{1,0:T(8,128)} custom-call(bf16[1,1,48,4096]{3,2,1,0:T(8,128)(2,1)} %acts.1, bf16[1,1,48,4608]{3,2,1,0:T(8,128)(2,1)} %base.1, bf16[1,4096,128]{2,1,0:T(8,128)(2,1)} %down.1, bf16[1,4608,128]{2,1,0:T(8,128)(2,1)} %up.1, bf16[1,4608]{1,0:T(2,128)(2,1)} %head.1, f32[36,128]{1,0:T(8,128)} %bitcast.2, s32[1,4]{1,0:T(1,128)} %lengths.1, ...), custom_call_target="tpu_custom_call" | custom-call | tf_op jit(solution)/shard_map/pallas_call | solution.py:548
  78.8 1.6 %shard_map.104 = (f32[1]{0:T(128)}, f32[1,128,128]{2,1,0:T(8,128)}, f32[1,144,128]{2,1,0:T(8,128)}) custom-call(f32[280,128]{1,0:T(8,128)} %shard_map.103.whole), custom_call_target="tpu_custom_call" | custom-call | tf_op jit(solution)/shard_map/pallas_call | solution.py:617

commit v6 on v5

--- a/solution.py
+++ b/solution.py
@@ -23,7 +23,7 @@
 WCH = 4
 OFFSETS = (0, 3, 1, 2)
 UNITS = ((0, 4), (1, 3), (2, -3), (3, 2), (3, -2), (2, 1), (1, -1), (0, 0))
-KA, KB = 2048, 2304
+KA, KB = 4096, 4608
 TN = (((0,), (0,)), ((), ()))
 NT = (((1,), (1,)), ((), ()))
 

time: 81.2 us -> 81.2 us (level)
  no operation moved by 1% of the time
where the time goes in v6:
time: 81.2 us; the launch traced here: 80.4 us
  Pallas kernels  79.7 us (98%)
    pallas_call x1, Pallas kernels, per_device(): pl.pallas_call(kernel, out_shape=jax.ShapeDtypeStruct((RAB + 8, RANK), F3...  78.2 us

profile of v6, /device:TPU:1, one launch (start us, length us, event | category | flops | bytes accessed | tf_op | source)
XLA Modules:
  0.0 80.4 jit_solution(16520938066864252458)
XLA Ops:
  0.6 78.2 %shard_map.103.whole = f32[280,128]{1,0:T(8,128)} custom-call(bf16[1,1,48,4096]{3,2,1,0:T(8,128)(2,1)} %acts.1, bf16[1,1,48,4608]{3,2,1,0:T(8,128)(2,1)} %base.1, bf16[1,4096,128]{2,1,0:T(8,128)(2,1)} %down.1, bf16[1,4608,128]{2,1,0:T(8,128)(2,1)} %up.1, bf16[1,4608]{1,0:T(2,128)(2,1)} %head.1, f32[36,128]{1,0:T(8,128)} %bitcast.2, s32[1,4]{1,0:T(1,128)} %lengths.1, ...), custom_call_target="tpu_custom_call" | custom-call | tf_op jit(solution)/shard_map/pallas_call | solution.py:548
  78.8 1.6 %shard_map.104 = (f32[1]{0:T(128)}, f32[1,128,128]{2,1,0:T(8,128)}, f32[1,144,128]{2,1,0:T(8,128)}) custom-call(f32[280,128]{1,0:T(8,128)} %shard_map.103.whole), custom_call_target="tpu_custom_call" | custom-call | tf_op jit(solution)/shard_map/pallas_call | solution.py:617
